TPU v7x, 128 devices: a whole 4x4x4 slice. The times are simulated.
128 devices in a mesh: seq: 32 (over y, z, core), head: 4 (over x).
Axes of the slice: x: 4, y: 4, z: 4, core: 2. Of those that a mesh axis runs over, the one named last changes fastest.
Arguments:
- query_rows: bfloat16 [32768, 5120], P(('seq', 'head')), may hold values from -6 to 6
- key_rows: bfloat16 [32768, 5120], P(('seq', 'head')), may hold values from -6 to 6
- value_rows: bfloat16 [32768, 5120], P(('seq', 'head')), may hold values from -6 to 6
- log_decay: bfloat16 [32768, 40], P(('seq', 'head')), may hold values from -1 to 0
- documents: int32 [32768], replicated, may hold values from 0 to 2, as said below
- norm_gain: float32 [5120], replicated, may hold values from 0.25 to 1.75
Outputs:
- attended: bfloat16 [32768, 5120], P(('seq', 'head'))
Inputs may be any that keep to these rules, and one draw needn't show every extreme that they name: `documents`: document numbers never fall along the tokens and each of the 3 numbers occurs.
All inputs are finite; a program needn't handle non-finite values.
Results may differ from a plain program's by a relative error of at most 0.0056.
Values may be sent and summed in bfloat16 or wider, within the bound.
No kernel may reach another device: no remote copies, remote signals or barrier semaphores. Data moves between devices by JAX's collectives and lax.ppermute only.
A program may use at most 640 MiB of HBM per device.

v0:
```python
import jax
import jax.numpy as jnp
from jax import lax
from jax.sharding import PartitionSpec as P

BLOCK = 256


def prefix(part, axis, combine, identity):
    place = lax.axis_index(axis)
    gathered = jax.tree.map(lambda a: lax.all_gather(a, axis), part)
    state = jax.tree.map(lambda a, e: jnp.zeros_like(a) + jnp.asarray(e, a.dtype), part, identity)

    def one(lap, state):
        return combine(
            state, jax.tree.map(lambda a: lax.dynamic_index_in_dim(a, lap, 0, False), gathered)
        )

    return lax.fori_loop(0, place, one, state)


def combine_states(earlier, later):
    return (earlier[0] * later[0], later[0][:, None, None] * earlier[1] + later[1])


def block_local(query_blocks, key_blocks, value_blocks, cumulative, doc_blocks):
    span = query_blocks.shape[1]
    scores = jnp.einsum(
        "nchd,nshd->nhcs", query_blocks, key_blocks, preferred_element_type=jnp.float32
    )
    cum_heads = jnp.swapaxes(cumulative, 1, 2)
    exponent = cum_heads[:, :, :, None] - cum_heads[:, :, None, :]
    causal = jnp.arange(span)[:, None] >= jnp.arange(span)[None, :]
    allowed = (causal[None] & (doc_blocks[:, :, None] == doc_blocks[:, None, :]))[:, None]
    decay_mask = jnp.where(allowed, jnp.exp(jnp.where(allowed, exponent, 0.0)), 0.0)
    weights = (scores * decay_mask).astype(jnp.bfloat16)
    return jnp.einsum("nhcs,nshd->nchd", weights, value_blocks, preferred_element_type=jnp.float32)


def attend(query, keyed, valued, decays, documents, first_row, gain_group, prefix_fn):
    row_count = query.shape[0]
    head_count = decays.shape[1]
    head_width = query.shape[1] // head_count
    block_count = row_count // BLOCK
    query_blocks = query.reshape(block_count, BLOCK, head_count, head_width)
    key_blocks = keyed.reshape(block_count, BLOCK, head_count, head_width)
    value_blocks = valued.reshape(block_count, BLOCK, head_count, head_width)
    cumulative = jnp.cumsum(
        decays.astype(jnp.float32).reshape(block_count, BLOCK, head_count), axis=1
    )
    local_docs = lax.dynamic_slice_in_dim(documents, first_row, row_count)
    doc_before = lax.dynamic_slice_in_dim(documents, jnp.maximum(first_row - 1, 0), 1)
    doc_blocks = local_docs.reshape(block_count, BLOCK)
    previous = jnp.concatenate([doc_before, doc_blocks[:-1, -1]])
    usable = (doc_blocks == previous[:, None]).astype(jnp.float32)
    final_cum = cumulative[:, -1, :]
    factor = jnp.exp(final_cum) * (doc_blocks[:, -1] == previous).astype(jnp.float32)[:, None]
    same_last = (doc_blocks == doc_blocks[:, -1:]).astype(jnp.float32)
    key_scale = jnp.exp(final_cum[:, None, :] - cumulative) * same_last[:, :, None]
    key_decayed = (key_blocks.astype(jnp.float32) * key_scale[..., None]).astype(jnp.bfloat16)
    block_state = jnp.einsum(
        "nchd,nche->nhde", key_decayed, value_blocks, preferred_element_type=jnp.float32
    )
    query_decayed = (
        query_blocks.astype(jnp.float32) * (jnp.exp(cumulative) * usable[:, :, None])[..., None]
    ).astype(jnp.bfloat16)

    def local_advance(carry, item):
        decay_so_far, state_so_far = carry
        block_factor, block_update = item
        return (
            (
                decay_so_far * block_factor,
                block_factor[:, None, None] * state_so_far + block_update,
            ),
            (decay_so_far, state_so_far),
        )

    start_carry = (
        jnp.ones((head_count,), jnp.float32),
        jnp.zeros((head_count, head_width, head_width), jnp.float32),
    )
    summary, entering = lax.scan(local_advance, start_carry, (factor, block_state))
    incoming = prefix_fn(summary)[1]

    def advance(carried_state, item):
        query_one, key_one, value_one, cum_one, doc_one, decayed_one, factor_one, update_one = item
        within = block_local(
            query_one[None], key_one[None], value_one[None], cum_one[None], doc_one[None]
        )[0]
        carried = jnp.einsum(
            "chd,hde->che",
            decayed_one,
            carried_state.astype(jnp.bfloat16),
            preferred_element_type=jnp.float32,
        )
        return (factor_one[:, None, None] * carried_state + update_one, within + carried)

    _, outputs = lax.scan(
        advance,
        incoming,
        (
            query_blocks,
            key_blocks,
            value_blocks,
            cumulative,
            doc_blocks,
            query_decayed,
            factor,
            block_state,
        ),
    )
    mean_square = jnp.mean(outputs * outputs, axis=-1, keepdims=True)
    normed = outputs * lax.rsqrt(mean_square + 1e-05) * gain_group.reshape(head_count, head_width)
    return normed.astype(jnp.bfloat16).reshape(row_count, head_count * head_width)


def body(query_rows, key_rows, value_rows, log_decay, documents, norm_gain):
    query, keyed, valued, decays = (
        lax.all_to_all(query_rows, "head", split_axis=1, concat_axis=0, tiled=True),
        lax.all_to_all(key_rows, "head", split_axis=1, concat_axis=0, tiled=True),
        lax.all_to_all(value_rows, "head", split_axis=1, concat_axis=0, tiled=True),
        lax.all_to_all(log_decay, "head", split_axis=1, concat_axis=0, tiled=True),
    )
    row_count = query.shape[0]
    group_width = query.shape[1]
    first_row = lax.axis_index("seq") * row_count
    gain_group = lax.dynamic_slice_in_dim(
        norm_gain, lax.axis_index("head") * group_width, group_width
    )

    def prefix_group(summary):
        identity = (jnp.ones_like(summary[0]), jnp.zeros_like(summary[1]))
        return prefix((summary[0], summary[1]), "seq", combine_states, identity)

    grouped = attend(query, keyed, valued, decays, documents, first_row, gain_group, prefix_group)
    return lax.all_to_all(grouped, "head", split_axis=0, concat_axis=1, tiled=True)


def solution(mesh):
    placed = (
        P(("seq", "head"), None),
        P(("seq", "head"), None),
        P(("seq", "head"), None),
        P(("seq", "head"), None),
        P(),
        P(),
    )
    return jax.shard_map(
        body, mesh=mesh, in_specs=placed, out_specs=P(("seq", "head"), None), check_vma=False
    )
```

profile of v0, /device:TPU:121, one launch (start us, length us, event | category | flops | bytes accessed | tf_op | source)
XLA Modules:
  0.0 299.5 jit_solution(4036128251627386428)
XLA Ops:
  6.5 1.4 all_to_all.60
  7.9 4.0 %all-to-all-start = ((bf16[256,4,10]{0,2,1:T(8,128)(2,1)}), bf16[256,4,10]{0,2,1:T(8,128)(2,1)S(1)}, u32[]{:S(2)}, u32[]{:S(2)}) async-start(bf16[256,4,10]{0,2,1:T(8,128)(2,1)} %all_to_all.60), calls=%async_computation | async-start | bytes 65536 | tf_op jit(solution)/shard_map/all_to_all | solution.py:123
  11.9 4.4 %copy.88 = bf16[256,5120]{0,1:T(8,128)(2,1)} copy(bf16[256,5120]{1,0:T(8,128)(2,1)} %param.13) | data formatting | bytes 5242880 | tf_op args[1]
  16.3 4.2 %all-to-all-start.1 = ((bf16[256,4,1280]{0,2,1:T(8,128)(2,1)}), bf16[256,4,1280]{0,2,1:T(8,128)(2,1)S(1)}, u32[]{:S(2)}, u32[]{:S(2)}) async-start(bf16[256,4,1280]{0,2,1:T(8,128)(2,1)} %bitcast.125), calls=%async_computation.1 | async-start | bytes 5242880 | tf_op jit(solution)/shard_map/all_to_all | solution.py:121
  20.5 4.4 %copy.91 = bf16[256,5120]{0,1:T(8,128)(2,1)} copy(bf16[256,5120]{1,0:T(8,128)(2,1)} %param.14) | data formatting | bytes 5242880 | tf_op args[2]
  24.9 26.1 %all-to-all-done.1 = bf16[256,4,1280]{0,2,1:T(8,128)(2,1)S(1)} async-done(((bf16[256,4,1280]{0,2,1:T(8,128)(2,1)}), bf16[256,4,1280]{0,2,1:T(8,128)(2,1)S(1)}, u32[]{:S(2)}, u32[]{:S(2)}) %all-to-all-start.1) | async-done | bytes 2621472 | tf_op jit(solution)/shard_map/all_to_all | solution.py:121
  51.0 1.5 copy-done.5
  52.5 4.6 %all-to-all-start.2 = ((bf16[256,4,1280]{0,2,1:T(8,128)(2,1)}), bf16[256,4,1280]{0,2,1:T(8,128)(2,1)}, u32[]{:S(2)}, u32[]{:S(2)}) async-start(bf16[256,4,1280]{0,2,1:T(8,128)(2,1)} %bitcast.123), calls=%async_computation.2 | async-start | bytes 5242880 | tf_op jit(solution)/shard_map/all_to_all | solution.py:122
  57.9 1.3 dynamic_slice.55
  61.4 2.3 reduce-window.6
  64.5 22.2 %all-to-all-done.2 = bf16[256,4,1280]{0,2,1:T(8,128)(2,1)} async-done(((bf16[256,4,1280]{0,2,1:T(8,128)(2,1)}), bf16[256,4,1280]{0,2,1:T(8,128)(2,1)}, u32[]{:S(2)}, u32[]{:S(2)}) %all-to-all-start.2) | async-done | bytes 2621472 | tf_op jit(solution)/shard_map/all_to_all | solution.py:122
  86.7 3.4 %fusion.27 = f32[4,10,128,128]{3,2,1,0:T(8,128)S(1)} fusion(bf16[4,256,10,128]{1,3,2,0:T(8,128)(2,1)} %bitcast.27, bf16[4,256,10,128]{1,3,2,0:T(8,128)(2,1)} %bitcast.119, f32[4,256,10]{1,2,0:T(8,128)S(1)} %copy.90), kind=kOutput, calls=%fused_computation.41 | convolution fusion | flops 339476480 | bytes 7905280 | tf_op jit(solution)/shard_map/nchd,nche->nhde/dot_general | solution.py:61
  91.7 4.6 %copy.93 = bf16[256,5120]{0,1:T(8,128)(2,1)} copy(bf16[256,5120]{1,0:T(8,128)(2,1)} %param.12) | data formatting | bytes 5242880 | tf_op args[0]
  96.3 3.8 %all-to-all-start.3 = ((bf16[256,4,1280]{0,2,1:T(8,128)(2,1)}), bf16[256,4,1280]{0,2,1:T(8,128)(2,1)S(1)}, u32[]{:S(2)}, u32[]{:S(2)}) async-start(bf16[256,4,1280]{0,2,1:T(8,128)(2,1)} %bitcast.124), calls=%async_computation.3 | async-start | bytes 5242880 | tf_op jit(solution)/shard_map/all_to_all | solution.py:120
  101.9 63.2 %all-reduce = f32[320]{0:T(512)S(1)} all-reduce(f32[320]{0:T(512)S(1)} %dynamic-update-slice), channel_id=2, replica_groups=mesh['seq'=32,'head'=4] {'seq'}, use_global_device_ids=true, to_apply=%add | all-reduce | flops 320 | bytes 2560
  165.2 2.3 multiply_convert_fusion.2
  167.5 7.4 %all-gather.4.cloned.1.call-done = f32[320,128,128]{2,1,0:T(8,128)} async-done(((f32[10,128,128]{2,1,0:T(8,128)}), f32[320,128,128]{2,1,0:T(8,128)}) %all-gather.4.cloned.1.call-update) | async-done | bytes 20971536 | tf_op jit(solution)/shard_map/all_gather | solution.py:11
  174.9 40.4 %while.37 = (s32[]{:T(128)}, f32[10,128,128]{2,1,0:T(8,128)S(1)}, s32[]{:T(128)}, f32[32,10]{1,0:T(8,128)S(1)}, f32[32,10,128,128]{3,2,1,0:T(8,128)}, /*index=5*/s32[]{:T(128)}, s32[]{:T(128)}, s32[]{:T(128)}) while((s32[]{:T(128)}, f32[10,128,128]{2,1,0:T(8,128)S(1)}, s32[]{:T(128)}, f32[32,10]{1,0:T(8,128)S(1)}, ...), condition=%wide.region_5.6_spmd, body=%wide.region_4.5_spmd.sunk | while | flops 327685 | bytes 1966327 | solution.py:19
  175.0 1.3 bitcast_add_fusion.6
  176.3 1.3 bitcast_add_fusion.6
  177.6 1.3 bitcast_add_fusion.6
  178.9 1.3 bitcast_add_fusion.6
  180.2 1.3 bitcast_add_fusion.6
  181.5 1.3 bitcast_add_fusion.6
  182.8 1.3 bitcast_add_fusion.6
  184.1 1.3 bitcast_add_fusion.6
  185.4 1.3 bitcast_add_fusion.6
  186.7 1.3 bitcast_add_fusion.6
  188.0 1.3 bitcast_add_fusion.6
  189.3 1.3 bitcast_add_fusion.6
  190.6 1.3 bitcast_add_fusion.6
  191.9 1.3 bitcast_add_fusion.6
  193.2 1.3 bitcast_add_fusion.6
  194.5 1.3 bitcast_add_fusion.6
  195.8 1.3 bitcast_add_fusion.6
  197.1 1.3 bitcast_add_fusion.6
  198.4 1.3 bitcast_add_fusion.6
  199.8 1.3 bitcast_add_fusion.6
  201.1 1.3 bitcast_add_fusion.6
  202.4 1.3 bitcast_add_fusion.6
  203.7 1.3 bitcast_add_fusion.6
  205.0 1.3 bitcast_add_fusion.6
  206.3 1.3 bitcast_add_fusion.6
  207.6 1.3 bitcast_add_fusion.6
  208.9 1.3 bitcast_add_fusion.6
  210.2 1.3 bitcast_add_fusion.6
  211.5 1.3 bitcast_add_fusion.6
  212.8 1.3 bitcast_add_fusion.6
  214.1 1.3 bitcast_add_fusion.6
  215.4 27.1 %while.38 = (s32[]{:T(128)}, f32[10,128,128]{2,1,0:T(8,128)S(1)}, f32[4,256,10,128]{1,3,2,0:T(8,128)}, f32[4,10]{1,0:T(4,128)S(1)}, f32[4,10,128,128]{3,2,1,0:T(...) while((s32[]{:T(128)}, f32[10,128,128]{2,1,0:T(8,128)S(1)}, ...), condition=%wide.region_7.8_spmd, body=%wide.region_6.7_spmd.sunk | while | flops 423723008 | bytes 9385725 | solution.py:99
  215.4 1.5 convolution_bitcast_fusion.3
  217.0 3.8 %fusion.48 = f32[4,256,10,128]{1,3,2,0:T(8,128)} fusion(f32[4,256,10,128]{1,3,2,0:T(8,128)} %get-tuple-element.454, s32[]{:T(128)} %get-tuple-element.452, f32[256,10,128]{0,2,1:T(8,128)S(1)} %convolution_bitcast_fusion.3, f32[10,256]{1,0:T(8,128)S(1)} %bitcast.130, pred[256,256]{1,0:T(8,128)(4,1)S(1)} %fusion.47, ...), kind=kOutput, calls=%fused_computation.6.clone.1 | convolution fusion | flops 339148800 | bytes 4687872 | tf_op jit(solution)/shard_map/while/body/eval_jaxpr/nhcs,nshd->nchd/dot_general | solution.py:37
  220.9 1.2 bitcast_add_fusion.7
  222.1 1.5 convolution_bitcast_fusion.3
  223.8 3.9 %fusion.48 = f32[4,256,10,128]{1,3,2,0:T(8,128)} fusion(f32[4,256,10,128]{1,3,2,0:T(8,128)} %get-tuple-element.454, s32[]{:T(128)} %get-tuple-element.452, f32[256,10,128]{0,2,1:T(8,128)S(1)} %convolution_bitcast_fusion.3, f32[10,256]{1,0:T(8,128)S(1)} %bitcast.130, pred[256,256]{1,0:T(8,128)(4,1)S(1)} %fusion.47, ...), kind=kOutput, calls=%fused_computation.6.clone.1 | convolution fusion | flops 339148800 | bytes 4687872 | tf_op jit(solution)/shard_map/while/body/eval_jaxpr/nhcs,nshd->nchd/dot_general | solution.py:37
  228.9 1.5 convolution_bitcast_fusion.3
  230.6 3.8 %fusion.48 = f32[4,256,10,128]{1,3,2,0:T(8,128)} fusion(f32[4,256,10,128]{1,3,2,0:T(8,128)} %get-tuple-element.454, s32[]{:T(128)} %get-tuple-element.452, f32[256,10,128]{0,2,1:T(8,128)S(1)} %convolution_bitcast_fusion.3, f32[10,256]{1,0:T(8,128)S(1)} %bitcast.130, pred[256,256]{1,0:T(8,128)(4,1)S(1)} %fusion.47, ...), kind=kOutput, calls=%fused_computation.6.clone.1 | convolution fusion | flops 339148800 | bytes 4687872 | tf_op jit(solution)/shard_map/while/body/eval_jaxpr/nhcs,nshd->nchd/dot_general | solution.py:37
  235.7 1.5 convolution_bitcast_fusion.3
  237.3 3.9 %fusion.48 = f32[4,256,10,128]{1,3,2,0:T(8,128)} fusion(f32[4,256,10,128]{1,3,2,0:T(8,128)} %get-tuple-element.454, s32[]{:T(128)} %get-tuple-element.452, f32[256,10,128]{0,2,1:T(8,128)S(1)} %convolution_bitcast_fusion.3, f32[10,256]{1,0:T(8,128)S(1)} %bitcast.130, pred[256,256]{1,0:T(8,128)(4,1)S(1)} %fusion.47, ...), kind=kOutput, calls=%fused_computation.6.clone.1 | convolution fusion | flops 339148800 | bytes 4687872 | tf_op jit(solution)/shard_map/while/body/eval_jaxpr/nhcs,nshd->nchd/dot_general | solution.py:37
  242.5 3.2 %multiply_reduce_fusion = f32[4,256,10]{1,2,0:T(8,128)S(1)} fusion(f32[4,256,10,128]{1,3,2,0:T(8,128)} %get-tuple-element.137), kind=kLoop, calls=%fused_computation.38 | loop fusion | flops 2611200 | bytes 5283840 | tf_op jit(solution)/shard_map/reduce_sum | solution.py:113
  247.2 2.6 copy.99
  249.8 35.9 %all_to_all.80 = bf16[4,256,1280]{2,1,0:T(8,128)(2,1)S(1)} all-to-all(bf16[4,256,1280]{2,1,0:T(8,128)(2,1)} %copy.99), channel_id=1, replica_groups=mesh['seq'=32,'head'=4] {'head'}, dimensions={0} | all-to-all | bytes 5242880 | tf_op jit(solution)/shard_map/all_to_all | solution.py:137
  285.7 2.5 copy.100
  288.2 4.4 %copy.101 = bf16[256,5120]{1,0:T(8,128)(2,1)} copy(bf16[256,5120]{0,1:T(8,128)(2,1)} %bitcast.126) | data formatting | bytes 5242880 | tf_op jit(solution)/shard_map/all_to_all | solution.py:137
  (118 shorter events, 13.2 us)
Async XLA Ops:
  6.5 95.0 %copy-start = (f32[5120]{0:T(1024)S(1)}, f32[5120]{0:T(1024)}, u32[]{:S(2)}) copy-start(f32[5120]{0:T(1024)} %param.17) | copy-start | bytes 61444
  7.9 8.4 %all-to-all-start = ((bf16[256,4,10]{0,2,1:T(8,128)(2,1)}), bf16[256,4,10]{0,2,1:T(8,128)(2,1)S(1)}, u32[]{:S(2)}, u32[]{:S(2)}) async-start(bf16[256,4,10]{0,2,1:T(8,128)(2,1)} %all_to_all.60), calls=%async_computation | async-start | bytes 65536 | tf_op jit(solution)/shard_map/all_to_all | solution.py:123
  16.3 34.7 %all-to-all-start.1 = ((bf16[256,4,1280]{0,2,1:T(8,128)(2,1)}), bf16[256,4,1280]{0,2,1:T(8,128)(2,1)S(1)}, u32[]{:S(2)}, u32[]{:S(2)}) async-start(bf16[256,4,1280]{0,2,1:T(8,128)(2,1)} %bitcast.125), calls=%async_computation.1 | async-start | bytes 5242880 | tf_op jit(solution)/shard_map/all_to_all | solution.py:121
  51.0 1.5 copy-start.5
  52.5 34.2 %all-to-all-start.2 = ((bf16[256,4,1280]{0,2,1:T(8,128)(2,1)}), bf16[256,4,1280]{0,2,1:T(8,128)(2,1)}, u32[]{:S(2)}, u32[]{:S(2)}) async-start(bf16[256,4,1280]{0,2,1:T(8,128)(2,1)} %bitcast.123), calls=%async_computation.2 | async-start | bytes 5242880 | tf_op jit(solution)/shard_map/all_to_all | solution.py:122
  57.1 117.8 %all-gather.4.cloned.1.call-start = ((), (), s32[]{:S(2)}) async-start(), calls=%async_computation.5 | async-start | bytes 21626880 | tf_op jit(solution)/shard_map/all_gather | solution.py:11
  90.8 0.9 copy-start.3
  90.8 5.5 %copy-start.2 = (f32[4,10,128,128]{3,2,1,0:T(8,128)}, f32[4,10,128,128]{3,2,1,0:T(8,128)S(1)}, u32[]{:S(2)}) copy-start(f32[4,10,128,128]{3,2,1,0:T(8,128)S(1)} %get-tuple-element.477) | copy-start | bytes 7864324
  96.3 3.8 %copy-start.7 = (u32[128]{0:T(128)S(1)}, u32[128]{0:T(128)}, u32[]{:S(2)}) copy-start(u32[128]{0:T(128)} %constant.83) | copy-start | bytes 1540
  96.3 68.9 %all-to-all-start.3 = ((bf16[256,4,1280]{0,2,1:T(8,128)(2,1)}), bf16[256,4,1280]{0,2,1:T(8,128)(2,1)S(1)}, u32[]{:S(2)}, u32[]{:S(2)}) async-start(bf16[256,4,1280]{0,2,1:T(8,128)(2,1)} %bitcast.124), calls=%async_computation.3 | async-start | bytes 5242880 | tf_op jit(solution)/shard_map/all_to_all | solution.py:120
  165.2 2.3 copy-start.6
  242.5 4.0 %copy-start.4 = (f32[4,256,10,128]{1,3,2,0:T(8,128)S(1)}, f32[4,256,10,128]{1,3,2,0:T(8,128)}, u32[]{:S(2)}) copy-start(f32[4,256,10,128]{1,3,2,0:T(8,128)} %get-tuple-element.137) | copy-start | bytes 15728644
  288.2 4.4 %copy-start.1 = (f32[5120]{0:T(1024)S(1)}, f32[5120]{0:T(1024)}, u32[]{:S(2)}) copy-start(f32[5120]{0:T(1024)} %param.17) | copy-start | bytes 61444
Sparse Core Ops, SparseCore 0:
  91.8 82.9 all-gather.3
where the time goes:
time: 302 us; the launch traced here: 299 us
  blocking collectives  99.1 us (33%)
  waiting for transfers between devices  55.6 us (18%)
  other arithmetic  55.5 us (18%)
  local copies, waits for them, and re-layouts  32 us (11%)
  matrix products  24.7 us (8%)
  starting transfers between devices  16.6 us (5%)
  between operations  14.4 us (5%)
    unnamed x1, blocking collectives  63.2 us
    add x31, other arithmetic, combine_states(): later[0][:, None, None] * earlier[1] + later[1]  38.9 us
    all_to_all x1, blocking collectives, body(): lax.all_to_all(grouped, 'head', split_axis=0, concat_axis=1, tiled=True)  35.9 us
    all_to_all x1, waiting for transfers between devices, body(): lax.all_to_all(key_rows, 'head', split_axis=1, concat_axis=0, tiled=True)  26.1 us
    all_to_all x1, waiting for transfers between devices, body(): lax.all_to_all(value_rows, 'head', split_axis=1, concat_axis=0, tiled=True)  22.2 us
    unnamed x22, local copies, waits for them, and re-layouts  17.4 us
    dot_general x4, matrix products, block_local(): jnp.einsum('nhcs,nshd->nchd', weights, value_blocks, preferred_element_ty...  15.5 us
    all_to_all x3, local copies, waits for them, and re-layouts, body(): lax.all_to_all(grouped, 'head', split_axis=0, concat_axis=1, tiled=True)  9.5 us
  transfers between devices with their start and end apart: 5, of which 3 were waited for; matrix products, arithmetic and copies ran while one was open for 8% of the time, Pallas kernels for 0%

commit v1 on v0

v1 whole, which is shorter than its diff:
```python
import functools

import jax
import jax.numpy as jnp
from jax import lax
from jax.experimental import pallas as pl
from jax.experimental.pallas import tpu as pltpu
from jax.sharding import PartitionSpec as P

BLOCK = 256
DH = 128
HEADS = 40
GROUPS = 8
PER = HEADS // GROUPS
SLABS = 16
DEVICES = GROUPS * SLABS
F32 = jnp.float32
BF16 = jnp.bfloat16
VMEM = 58 << 20


def doc_row(docs_ref, block):
    rows = docs_ref[pl.ds(2 * block, 2), :]
    row = jnp.concatenate([rows[0:1], rows[1:2]], axis=1)
    before = docs_ref[pl.ds(jnp.maximum(2 * block - 1, 0), 1), :]
    prev = jnp.where(block == 0, row[:, 0:1], before[:, DH - 1 : DH])
    return row, prev


def lower_ones():
    t = lax.broadcasted_iota(jnp.int32, (BLOCK, BLOCK), 0)
    s = lax.broadcasted_iota(jnp.int32, (BLOCK, BLOCK), 1)
    return t >= s


def cum_rows(decay):
    tri = lower_ones().astype(F32).astype(BF16)
    return lax.dot_general(decay, tri, (((1,), (1,)), ((), ())), preferred_element_type=F32)


def state_kernel(block_ref, key_ref, value_ref, decay_ref, docs_ref, out_ref, scale_ref, factor_ref):
    group = pl.program_id(0)

    @pl.when(group == 0)
    def _():
        row, prev = doc_row(docs_ref, block_ref[0])
        last = row[:, BLOCK - 1 : BLOCK]
        cum = cum_rows(decay_ref[...])
        final = cum[:, BLOCK - 1 : BLOCK]
        same = (row == last).astype(F32)
        scale_ref[...] = jnp.exp(final - cum) * same
        factor = jnp.exp(final) * (last == prev).astype(F32)
        factor = jnp.broadcast_to(factor, (HEADS, DH))
        high = factor.astype(BF16).astype(F32)
        middle = (factor - high).astype(BF16).astype(F32)
        low = factor - high - middle
        lane = lax.broadcasted_iota(jnp.int32, (HEADS, DH), 1)
        parts = jnp.where(lane == 0, high, jnp.where(lane == 1, middle, jnp.where(lane == 2, low, 0.0)))
        factor_ref[0:HEADS, :] = parts
        factor_ref[HEADS:, :] = jnp.zeros((8, DH), F32)

    for one in range(PER):
        cols = slice(one * DH, (one + 1) * DH)
        keys = key_ref[:, cols].T.astype(F32)
        decayed = (keys * scale_ref[pl.ds(group * PER + one, 1), :]).astype(BF16)
        update = jnp.dot(decayed, value_ref[:, cols], preferred_element_type=F32)
        out_ref[:, one] = update.reshape(SLABS, 8, DH).astype(BF16)
    parts = factor_ref[pl.ds(group * PER, 8), :].astype(BF16)
    out_ref[:, PER] = jnp.broadcast_to(parts[None], (SLABS, 8, DH))


def scan_kernel(update_ref, out_ref, carry_ref):
    step = pl.program_id(0)

    @pl.when(step == 0)
    def _():
        carry_ref[...] = jnp.zeros_like(carry_ref)

    state = [carry_ref[one] for one in range(PER)]
    for b in range(update_ref.shape[0]):
        factors = jnp.sum(update_ref[b, PER].astype(F32), axis=1, keepdims=True)
        for one in range(PER):
            out_ref[b, one] = state[one].astype(BF16)
            state[one] = factors[one : one + 1] * state[one] + update_ref[b, one].astype(F32)
    for one in range(PER):
        carry_ref[one] = state[one]


def local_kernel(
    block_ref, query_ref, key_ref, value_ref, decay_ref, docs_ref, within_ref, decayed_ref, row_ref, col_ref, use_ref, mask_ref
):
    group = pl.program_id(0)

    @pl.when(group == 0)
    def _():
        row, prev = doc_row(docs_ref, block_ref[0])
        decay = decay_ref[...]
        row_ref[...] = cum_rows(decay)
        lower = lower_ones()
        ones = lower.astype(F32).astype(BF16)
        cum = lax.dot_general(ones, decay, (((1,), (1,)), ((), ())), preferred_element_type=F32)
        rows = jnp.broadcast_to(row.astype(F32), (BLOCK, BLOCK))
        cols = rows.T
        mask_ref[...] = (lower & (rows == cols)).astype(F32)
        usable = (cols[:, 0:1] == prev.astype(F32)).astype(F32)
        use = jnp.exp(cum) * usable
        for g in range(GROUPS):
            col_ref[g] = cum[:, g * PER : (g + 1) * PER]
            use_ref[g] = use[:, g * PER : (g + 1) * PER]

    allowed = mask_ref[...] > 0.5
    for one in range(PER):
        cols = slice(one * DH, (one + 1) * DH)
        query = query_ref[:, cols]
        scores = lax.dot_general(query, key_ref[:, cols], (((1,), (1,)), ((), ())), preferred_element_type=F32)
        exponent = col_ref[group, :, one : one + 1] - row_ref[pl.ds(group * PER + one, 1), :]
        mask = jnp.exp(jnp.where(allowed, exponent, -jnp.inf))
        weights = (scores * mask).astype(BF16)
        within_ref[:, cols] = jnp.dot(weights, value_ref[:, cols], preferred_element_type=F32)
        decayed_ref[:, cols] = (query.astype(F32) * use_ref[group, :, one : one + 1]).astype(BF16)


def finish_kernel(decayed_ref, state_ref, within_ref, gain_ref, out_ref):
    for one in range(PER):
        cols = slice(one * DH, (one + 1) * DH)
        state = state_ref[:, one].reshape(DH, DH)
        total = within_ref[:, cols] + jnp.dot(decayed_ref[:, cols], state, preferred_element_type=F32)
        square = jnp.mean(total * total, axis=1, keepdims=True)
        out_ref[:, cols] = (total * lax.rsqrt(square + 1e-05) * gain_ref[:, cols]).astype(BF16)


def body(query, keyed, valued, decay, documents, gain):
    axes = ("seq", "head")
    block = lax.axis_index(axes).astype(jnp.int32).reshape(1)
    docs = documents.reshape(-1, DH)
    gain = gain.reshape(1, -1)
    decay = decay.T
    wide = PER * DH
    rows = pl.BlockSpec((BLOCK, wide), lambda g, *_: (0, g))
    whole = lambda a: pl.BlockSpec(a.shape, lambda g, *_: (0,) * a.ndim)

    update = pl.pallas_call(
        state_kernel,
        grid_spec=pltpu.PrefetchScalarGridSpec(
            num_scalar_prefetch=1,
            grid=(GROUPS,),
            in_specs=[rows, rows, whole(decay), whole(docs)],
            out_specs=pl.BlockSpec((SLABS, PER + 1, 8, DH), lambda g, *_: (g, 0, 0, 0)),
            scratch_shapes=[pltpu.VMEM((HEADS, BLOCK), F32), pltpu.VMEM((HEADS + 8, DH), F32)],
        ),
        out_shape=jax.ShapeDtypeStruct((DEVICES, PER + 1, 8, DH), BF16),
        compiler_params=pltpu.CompilerParams(vmem_limit_bytes=VMEM),
        cost_estimate=pl.CostEstimate(flops=340_000_000, bytes_accessed=7_000_000, transcendentals=10_000),
        name="state_update",
    )(block, keyed, valued, decay, docs)

    moved = lax.all_to_all(update, axes, split_axis=0, concat_axis=0, tiled=True)

    within, decayed = pl.pallas_call(
        local_kernel,
        grid_spec=pltpu.PrefetchScalarGridSpec(
            num_scalar_prefetch=1,
            grid=(GROUPS,),
            in_specs=[rows, rows, rows, whole(decay), whole(docs)],
            out_specs=[rows, rows],
            scratch_shapes=[
                pltpu.VMEM((HEADS, BLOCK), F32),
                pltpu.VMEM((GROUPS, BLOCK, PER), F32),
                pltpu.VMEM((GROUPS, BLOCK, PER), F32),
                pltpu.VMEM((BLOCK, BLOCK), F32),
            ],
        ),
        out_shape=[jax.ShapeDtypeStruct(query.shape, F32), jax.ShapeDtypeStruct(query.shape, BF16)],
        compiler_params=pltpu.CompilerParams(vmem_limit_bytes=VMEM),
        cost_estimate=pl.CostEstimate(flops=1_400_000_000, bytes_accessed=16_000_000, transcendentals=2_700_000),
        name="local_attention",
    )(block, query, keyed, valued, decay, docs)

    chunk = 16
    states = pl.pallas_call(
        scan_kernel,
        grid=(DEVICES // chunk,),
        in_specs=[pl.BlockSpec((chunk, PER + 1, 8, DH), lambda b: (b, 0, 0, 0))],
        out_specs=pl.BlockSpec((chunk, PER, 8, DH), lambda b: (b, 0, 0, 0)),
        out_shape=jax.ShapeDtypeStruct((DEVICES, PER, 8, DH), BF16),
        scratch_shapes=[pltpu.VMEM((PER, 8, DH), F32)],
        compiler_params=pltpu.CompilerParams(vmem_limit_bytes=VMEM),
        name="block_scan",
    )(moved)

    entering = lax.all_to_all(states, axes, split_axis=0, concat_axis=0, tiled=True)

    return pl.pallas_call(
        finish_kernel,
        grid=(GROUPS,),
        in_specs=[
            rows,
            pl.BlockSpec((SLABS, PER, 8, DH), lambda g: (g, 0, 0, 0)),
            rows,
            pl.BlockSpec((1, wide), lambda g: (0, g)),
        ],
        out_specs=rows,
        out_shape=jax.ShapeDtypeStruct(query.shape, BF16),
        compiler_params=pltpu.CompilerParams(vmem_limit_bytes=VMEM),
        name="finish",
    )(decayed, entering, within, gain)


def solution(mesh):
    placed = P(("seq", "head"), None)
    return jax.shard_map(
        body, mesh=mesh, in_specs=(placed, placed, placed, placed, P(), P()), out_specs=placed, check_vma=False
    )
```

time: 302 us -> 87.3 us (0.29)
  the two profiles are of different devices: /device:TPU:121 before, /device:TPU:1 now
where the time goes in v1:
time: 87.3 us; the launch traced here: 86.4 us
  blocking collectives  37 us (42%)
  Pallas kernels  33.2 us (38%)
  waiting for transfers between devices  11.4 us (13%)
  starting transfers between devices  3.67 us (4%)
  local copies, waits for them, and re-layouts  1.14 us (1%)
    all_to_all x1, blocking collectives, body(): lax.all_to_all(update, axes, split_axis=0, concat_axis=0, tiled=True)  37 us
    all_to_all x1, waiting for transfers between devices, body(): lax.all_to_all(states, axes, split_axis=0, concat_axis=0, tiled=True)  11.4 us
    pallas_call x1, Pallas kernels, body(): pl.pallas_call(local_kernel, grid_spec=pltpu.PrefetchScalarGridSpec(num_s...  11.3 us
    pallas_call x1, Pallas kernels, body(): pl.pallas_call(finish_kernel, grid=(GROUPS,), in_specs=[rows, pl.BlockSpe...  8.63 us
    pallas_call x1, Pallas kernels, body(): pl.pallas_call(state_kernel, grid_spec=pltpu.PrefetchScalarGridSpec(num_s...  7.48 us
    pallas_call x1, Pallas kernels, body(): pl.pallas_call(scan_kernel, grid=(DEVICES // chunk,), in_specs=[pl.BlockS...  5.78 us
    all_to_all x1, starting transfers between devices, body(): lax.all_to_all(states, axes, split_axis=0, concat_axis=0, tiled=True)  3.67 us
  transfers between devices with their start and end apart: 1, of which 1 were waited for; matrix products, arithmetic and copies ran while one was open for 0% of the time, Pallas kernels for 13%

profile of v1, /device:TPU:1, one launch (start us, length us, event | category | flops | bytes accessed | tf_op | source)
XLA Modules:
  0.0 86.4 jit_solution(2871958905017530318)
XLA Ops:
  0.0 7.5 %state_update.1 = bf16[128,6,8,128]{3,2,1,0:T(8,128)(2,1)} custom-call(s32[1]{0:T(128)} %bitcast.block_ref, bf16[256,5120]{1,0:T(8,128)(2,1)} %key_ref.3, bf16[256,5120]{1,0:T(8,128)(2,1)} %value_ref.3, bf16[40,256]{1,0:T(8,128)(2,1)} %bitcast.6, s32[256,128]{1,0:T(8,128)} %bitcast.4), custom_call_target="tpu_custom_call" | custom-call | flops 340000000 | bytes 7000000 | tf_op jit(solution)/shard_map/state_update/pallas_call | solution.py:142
  7.5 37.0 %all_to_all.10.update_ref = bf16[128,6,8,128]{3,2,1,0:T(8,128)(2,1)} all-to-all(bf16[128,6,8,128]{3,2,1,0:T(8,128)(2,1)} %state_update.1), channel_id=1, replica_groups=mesh['seq'=32,'head'=4] {'seq','head'}, dimensions={0} | all-to-all | bytes 3145728 | tf_op jit(solution)/shard_map/all_to_all | solution.py:157
  44.5 5.8 %block_scan.1 = bf16[128,5,8,128]{3,2,1,0:T(8,128)(2,1)} custom-call(bf16[128,6,8,128]{3,2,1,0:T(8,128)(2,1)} %all_to_all.10.update_ref), custom_call_target="tpu_custom_call" | custom-call | tf_op jit(solution)/shard_map/block_scan/pallas_call | solution.py:180
  50.2 3.7 %all-to-all-start.1 = ((bf16[128,5,8,128]{3,2,1,0:T(8,128)(2,1)}), bf16[128,5,8,128]{3,2,1,0:T(8,128)(2,1)S(1)}, u32[]{:S(2)}, u32[]{:S(2)}) async-start(bf16[128,5,8,128]{3,2,1,0:T(8,128)(2,1)} %block_scan.1), calls=%async_computation.1 | async-start | bytes 2621440 | tf_op jit(solution)/shard_map/all_to_all | solution.py:191
  53.9 11.3 %local_attention.1 = (f32[256,5120]{1,0:T(8,128)}, bf16[256,5120]{1,0:T(8,128)(2,1)}) custom-call(s32[1]{0:T(128)} %bitcast.block_ref, bf16[256,5120]{1,0:T(8,128)(2,1)} %query_ref.1, bf16[256,5120]{1,0:T(8,128)(2,1)} %key_ref.3, bf16[256,5120]{1,0:T(8,128)(2,1)} %value_ref.3, bf16[40,256]{1,0:T(8,128)(2,1)} %bitcast.7, s32[256,128]{1,0:T(8,128)} %bitcast.5), custom_call_target="tpu_custom_call" | custom-call | flops 1400000000 | bytes 16000000 | tf_op jit(solution)/shard_map/local_attention/pallas_call | solution.py:159
  65.3 11.4 %all-to-all-done.1.state_ref = bf16[128,5,8,128]{3,2,1,0:T(8,128)(2,1)S(1)} async-done(((bf16[128,5,8,128]{3,2,1,0:T(8,128)(2,1)}), bf16[128,5,8,128]{3,2,1,0:T(8,128)(2,1)S(1)}, u32[]{:S(2)}, u32[]{:S(2)}) %all-to-all-start.1) | async-done | bytes 1310752 | tf_op jit(solution)/shard_map/all_to_all | solution.py:191
  76.6 0.0 copy-start
  76.6 1.1 %copy-done = bf16[128,5,8,128]{3,2,1,0:T(8,128)(2,1)} copy-done((bf16[128,5,8,128]{3,2,1,0:T(8,128)(2,1)}, bf16[128,5,8,128]{3,2,1,0:T(8,128)(2,1)S(1)}, u32[]{:S(2)}) %copy-start) | copy-done | bytes 1310744
  77.8 8.6 %finish.1 = bf16[256,5120]{1,0:T(8,128)(2,1)} custom-call(bf16[256,5120]{1,0:T(8,128)(2,1)} %get-tuple-element.7.decayed_ref, bf16[128,5,8,128]{3,2,1,0:T(8,128)(2,1)} %copy-done, f32[256,5120]{1,0:T(8,128)} %get-tuple-element.8.within_ref, f32[1,5120]{1,0:T(1,128)} %bitcast.8), custom_call_target="tpu_custom_call" | custom-call | tf_op jit(solution)/shard_map/finish/pallas_call | solution.py:193
Async XLA Ops:
  50.2 26.4 %all-to-all-start.1 = ((bf16[128,5,8,128]{3,2,1,0:T(8,128)(2,1)}), bf16[128,5,8,128]{3,2,1,0:T(8,128)(2,1)S(1)}, u32[]{:S(2)}, u32[]{:S(2)}) async-start(bf16[128,5,8,128]{3,2,1,0:T(8,128)(2,1)} %block_scan.1), calls=%async_computation.1 | async-start | bytes 2621440 | tf_op jit(solution)/shard_map/all_to_all | solution.py:191
  76.6 1.1 %copy-start = (bf16[128,5,8,128]{3,2,1,0:T(8,128)(2,1)}, bf16[128,5,8,128]{3,2,1,0:T(8,128)(2,1)S(1)}, u32[]{:S(2)}) copy-start(bf16[128,5,8,128]{3,2,1,0:T(8,128)(2,1)S(1)} %all-to-all-done.1.state_ref) | copy-start | bytes 3932164

commit v2 on v1

--- a/solution.py
+++ b/solution.py
@@ -14,6 +14,7 @@
 PER = HEADS // GROUPS
 SLABS = 16
 DEVICES = GROUPS * SLABS
+STEP_GROUPS = 4
 F32 = jnp.float32
 BF16 = jnp.bfloat16
 VMEM = 58 << 20
@@ -39,9 +40,9 @@
 
 
 def state_kernel(block_ref, key_ref, value_ref, decay_ref, docs_ref, out_ref, scale_ref, factor_ref):
-    group = pl.program_id(0)
-
-    @pl.when(group == 0)
+    step = pl.program_id(0)
+
+    @pl.when(step == 0)
     def _():
         row, prev = doc_row(docs_ref, block_ref[0])
         last = row[:, BLOCK - 1 : BLOCK]
@@ -59,31 +60,29 @@
         factor_ref[0:HEADS, :] = parts
         factor_ref[HEADS:, :] = jnp.zeros((8, DH), F32)
 
-    for one in range(PER):
-        cols = slice(one * DH, (one + 1) * DH)
-        keys = key_ref[:, cols].T.astype(F32)
-        decayed = (keys * scale_ref[pl.ds(group * PER + one, 1), :]).astype(BF16)
-        update = jnp.dot(decayed, value_ref[:, cols], preferred_element_type=F32)
-        out_ref[:, one] = update.reshape(SLABS, 8, DH).astype(BF16)
-    parts = factor_ref[pl.ds(group * PER, 8), :].astype(BF16)
-    out_ref[:, PER] = jnp.broadcast_to(parts[None], (SLABS, 8, DH))
-
-
-def scan_kernel(update_ref, out_ref, carry_ref):
-    step = pl.program_id(0)
-
-    @pl.when(step == 0)
-    def _():
-        carry_ref[...] = jnp.zeros_like(carry_ref)
-
-    state = [carry_ref[one] for one in range(PER)]
-    for b in range(update_ref.shape[0]):
+    for sub in range(STEP_GROUPS):
+        first = (step * STEP_GROUPS + sub) * PER
+        slabs = slice(sub * SLABS, (sub + 1) * SLABS)
+        for one in range(PER):
+            cols = slice((sub * PER + one) * DH, (sub * PER + one + 1) * DH)
+            keys = key_ref[:, cols].T.astype(F32)
+            decayed = (keys * scale_ref[pl.ds(first + one, 1), :]).astype(BF16)
+            update = jnp.dot(decayed, value_ref[:, cols], preferred_element_type=F32)
+            out_ref[slabs, one] = update.reshape(SLABS, 8, DH).astype(BF16)
+        parts = factor_ref[pl.ds(first, 8), :].astype(BF16)
+        out_ref[slabs, PER] = jnp.broadcast_to(parts[None], (SLABS, 8, DH))
+
+
+def scan_kernel(update_ref, decayed_hbm, out_ref, decayed_ref, sem):
+    fetch = pltpu.make_async_copy(decayed_hbm, decayed_ref, sem)
+    fetch.start()
+    state = [jnp.zeros((8, DH), F32) for _ in range(PER)]
+    for b in range(DEVICES):
         factors = jnp.sum(update_ref[b, PER].astype(F32), axis=1, keepdims=True)
         for one in range(PER):
             out_ref[b, one] = state[one].astype(BF16)
             state[one] = factors[one : one + 1] * state[one] + update_ref[b, one].astype(F32)
-    for one in range(PER):
-        carry_ref[one] = state[one]
+    fetch.wait()
 
 
 def local_kernel(
@@ -120,13 +119,21 @@
         decayed_ref[:, cols] = (query.astype(F32) * use_ref[group, :, one : one + 1]).astype(BF16)
 
 
-def finish_kernel(decayed_ref, state_ref, within_ref, gain_ref, out_ref):
-    for one in range(PER):
-        cols = slice(one * DH, (one + 1) * DH)
-        state = state_ref[:, one].reshape(DH, DH)
-        total = within_ref[:, cols] + jnp.dot(decayed_ref[:, cols], state, preferred_element_type=F32)
-        square = jnp.mean(total * total, axis=1, keepdims=True)
-        out_ref[:, cols] = (total * lax.rsqrt(square + 1e-05) * gain_ref[:, cols]).astype(BF16)
+def finish_kernel(decayed_ref, state_ref, within_ref, gain_ref, out_hbm, out_ref, sems):
+    copies = []
+    for g in range(GROUPS):
+        for one in range(g * PER, (g + 1) * PER):
+            cols = slice(one * DH, (one + 1) * DH)
+            state = state_ref[g * SLABS : (g + 1) * SLABS, one - g * PER].reshape(DH, DH)
+            carried = jnp.dot(decayed_ref[:, cols], state, preferred_element_type=F32)
+            total = within_ref[:, cols] + carried
+            square = jnp.mean(total * total, axis=1, keepdims=True)
+            out_ref[:, cols] = (total * lax.rsqrt(square + 1e-05) * gain_ref[:, cols]).astype(BF16)
+        cols = slice(g * PER * DH, (g + 1) * PER * DH)
+        copies.append(pltpu.make_async_copy(out_ref.at[:, cols], out_hbm.at[:, cols], sems.at[g]))
+        copies[-1].start()
+    for copy in copies:
+        copy.wait()
 
 
 def body(query, keyed, valued, decay, documents, gain):
@@ -139,13 +146,14 @@
     rows = pl.BlockSpec((BLOCK, wide), lambda g, *_: (0, g))
     whole = lambda a: pl.BlockSpec(a.shape, lambda g, *_: (0,) * a.ndim)
 
+    wider = pl.BlockSpec((BLOCK, STEP_GROUPS * wide), lambda g, *_: (0, g))
     update = pl.pallas_call(
         state_kernel,
         grid_spec=pltpu.PrefetchScalarGridSpec(
             num_scalar_prefetch=1,
-            grid=(GROUPS,),
-            in_specs=[rows, rows, whole(decay), whole(docs)],
-            out_specs=pl.BlockSpec((SLABS, PER + 1, 8, DH), lambda g, *_: (g, 0, 0, 0)),
+            grid=(GROUPS // STEP_GROUPS,),
+            in_specs=[wider, wider, whole(decay), whole(docs)],
+            out_specs=pl.BlockSpec((STEP_GROUPS * SLABS, PER + 1, 8, DH), lambda g, *_: (g, 0, 0, 0)),
             scratch_shapes=[pltpu.VMEM((HEADS, BLOCK), F32), pltpu.VMEM((HEADS + 8, DH), F32)],
         ),
         out_shape=jax.ShapeDtypeStruct((DEVICES, PER + 1, 8, DH), BF16),
@@ -176,32 +184,27 @@
         name="local_attention",
     )(block, query, keyed, valued, decay, docs)
 
-    chunk = 16
-    states = pl.pallas_call(
+    moved, within, decayed = lax.optimization_barrier((moved, within, decayed))
+    vmem = pl.BlockSpec(memory_space=pltpu.VMEM)
+    states, decayed = pl.pallas_call(
         scan_kernel,
-        grid=(DEVICES // chunk,),
-        in_specs=[pl.BlockSpec((chunk, PER + 1, 8, DH), lambda b: (b, 0, 0, 0))],
-        out_specs=pl.BlockSpec((chunk, PER, 8, DH), lambda b: (b, 0, 0, 0)),
-        out_shape=jax.ShapeDtypeStruct((DEVICES, PER, 8, DH), BF16),
-        scratch_shapes=[pltpu.VMEM((PER, 8, DH), F32)],
-        compiler_params=pltpu.CompilerParams(vmem_limit_bytes=VMEM),
+        in_specs=[vmem, pl.BlockSpec(memory_space=pltpu.HBM)],
+        out_specs=[vmem, vmem],
+        out_shape=[jax.ShapeDtypeStruct((DEVICES, PER, 8, DH), BF16), jax.ShapeDtypeStruct(query.shape, BF16)],
+        scratch_shapes=[pltpu.SemaphoreType.DMA],
+        compiler_params=pltpu.CompilerParams(vmem_limit_bytes=8 << 20),
         name="block_scan",
-    )(moved)
+    )(moved, pltpu.with_memory_space_constraint(decayed, pltpu.HBM))
 
     entering = lax.all_to_all(states, axes, split_axis=0, concat_axis=0, tiled=True)
 
     return pl.pallas_call(
         finish_kernel,
-        grid=(GROUPS,),
-        in_specs=[
-            rows,
-            pl.BlockSpec((SLABS, PER, 8, DH), lambda g: (g, 0, 0, 0)),
-            rows,
-            pl.BlockSpec((1, wide), lambda g: (0, g)),
-        ],
-        out_specs=rows,
+        in_specs=[vmem] * 4,
+        out_specs=pl.BlockSpec(memory_space=pl.ANY),
         out_shape=jax.ShapeDtypeStruct(query.shape, BF16),
-        compiler_params=pltpu.CompilerParams(vmem_limit_bytes=VMEM),
+        scratch_shapes=[pltpu.VMEM(query.shape, BF16), pltpu.SemaphoreType.DMA((GROUPS,))],
+        compiler_params=pltpu.CompilerParams(vmem_limit_bytes=16 << 20),
         name="finish",
     )(decayed, entering, within, gain)
 

time: 87.3 us -> 71.7 us (0.82)
  Pallas kernels: 33.2 us -> 19.8 us
  blocking collectives: 37 us -> 25.9 us
  starting transfers between devices: 3.67 us -> 11.5 us
  waiting for transfers between devices: 11.4 us -> 14.1 us
  local copies, waits for them, and re-layouts: 1.14 us -> 0.01 us
    all_to_all x1, blocking collectives: 37 us -> 25.9 us  [body(): lax.all_to_all(states, axes, split_axis=0, concat_axis=0, tiled=True)]
    pallas_call x2, Pallas kernels: 14.4 us -> 4.47 us  [the longest x1 2.57 us: body(): pl.pallas_call(finish_kernel, in_specs=[vmem] * 4, out_specs=pl.BlockSpec...]
    all_to_all x1, starting transfers between devices: 3.67 us -> 11.5 us  [body(): lax.all_to_all(update, axes, split_axis=0, concat_axis=0, tiled=True)]
    pallas_call x1, Pallas kernels: 7.48 us -> 4.07 us  [body(): pl.pallas_call(state_kernel, grid_spec=pltpu.PrefetchScalarGridSpec(num_s...]
    all_to_all x1, waiting for transfers between devices: 11.4 us -> 14.1 us  [body(): lax.all_to_all(update, axes, split_axis=0, concat_axis=0, tiled=True)]
    unnamed x2 -> x4, local copies, waits for them, and re-layouts: 1.14 us -> 0.01 us
  transfers between devices with their start and end apart: 1 -> 1, of which waited for: 1 -> 1; matrix products, arithmetic and copies ran while one was open for 0% -> 0% of each run, Pallas kernels for 13% -> 16%
where the time goes in v2:
time: 71.7 us; the launch traced here: 71.3 us
  blocking collectives  25.9 us (36%)
  Pallas kernels  19.8 us (28%)
  waiting for transfers between devices  14.1 us (20%)
  starting transfers between devices  11.5 us (16%)
    all_to_all x1, blocking collectives, body(): lax.all_to_all(states, axes, split_axis=0, concat_axis=0, tiled=True)  25.9 us
    all_to_all x1, waiting for transfers between devices, body(): lax.all_to_all(update, axes, split_axis=0, concat_axis=0, tiled=True)  14.1 us
    all_to_all x1, starting transfers between devices, body(): lax.all_to_all(update, axes, split_axis=0, concat_axis=0, tiled=True)  11.5 us
    pallas_call x1, Pallas kernels, body(): pl.pallas_call(local_kernel, grid_spec=pltpu.PrefetchScalarGridSpec(num_s...  11.3 us
    pallas_call x1, Pallas kernels, body(): pl.pallas_call(state_kernel, grid_spec=pltpu.PrefetchScalarGridSpec(num_s...  4.07 us
    pallas_call x1, Pallas kernels, body(): pl.pallas_call(finish_kernel, in_specs=[vmem] * 4, out_specs=pl.BlockSpec...  2.57 us
    pallas_call x1, Pallas kernels, body(): pl.pallas_call(scan_kernel, in_specs=[vmem, pl.BlockSpec(memory_space=plt...  1.9 us
  transfers between devices with their start and end apart: 1, of which 1 were waited for; matrix products, arithmetic and copies ran while one was open for 0% of the time, Pallas kernels for 16%

profile of v2, /device:TPU:1, one launch (start us, length us, event | category | flops | bytes accessed | tf_op | source)
XLA Modules:
  0.0 71.3 jit_solution(12513416576745844874)
XLA Ops:
  0.0 4.1 %state_update.1 = bf16[128,6,8,128]{3,2,1,0:T(8,128)(2,1)} custom-call(s32[1]{0:T(128)} %bitcast.block_ref, bf16[256,5120]{1,0:T(8,128)(2,1)} %key_ref.3, bf16[256,5120]{1,0:T(8,128)(2,1)} %value_ref.3, bf16[40,256]{1,0:T(8,128)(2,1)} %bitcast.7, s32[256,128]{1,0:T(8,128)} %bitcast.5), custom_call_target="tpu_custom_call" | custom-call | flops 340000000 | bytes 7000000 | tf_op jit(solution)/shard_map/state_update/pallas_call | solution.py:150
  4.1 11.5 %all-to-all-start = ((bf16[128,6,8,128]{3,2,1,0:T(8,128)(2,1)}), bf16[128,6,8,128]{3,2,1,0:T(8,128)(2,1)S(1)}, u32[]{:S(2)}, u32[]{:S(2)}) async-start(bf16[128,6,8,128]{3,2,1,0:T(8,128)(2,1)} %state_update.1), calls=%async_computation | async-start | bytes 3145728 | tf_op jit(solution)/shard_map/all_to_all | solution.py:165
  15.6 11.3 %local_attention.1 = (f32[256,5120]{1,0:T(8,128)}, bf16[256,5120]{1,0:T(8,128)(2,1)}) custom-call(s32[1]{0:T(128)} %bitcast.block_ref, bf16[256,5120]{1,0:T(8,128)(2,1)} %query_ref.1, bf16[256,5120]{1,0:T(8,128)(2,1)} %key_ref.3, bf16[256,5120]{1,0:T(8,128)(2,1)} %value_ref.3, bf16[40,256]{1,0:T(8,128)(2,1)} %bitcast.8, s32[256,128]{1,0:T(8,128)} %bitcast.6), custom_call_target="tpu_custom_call" | custom-call | flops 1400000000 | bytes 16000000 | tf_op jit(solution)/shard_map/local_attention/pallas_call | solution.py:167
  26.9 14.1 %all-to-all-done.update_ref = bf16[128,6,8,128]{3,2,1,0:T(8,128)(2,1)S(1)} async-done(((bf16[128,6,8,128]{3,2,1,0:T(8,128)(2,1)}), bf16[128,6,8,128]{3,2,1,0:T(8,128)(2,1)S(1)}, u32[]{:S(2)}, u32[]{:S(2)}) %all-to-all-start) | async-done | bytes 1572896 | tf_op jit(solution)/shard_map/all_to_all | solution.py:165
  40.9 0.0 copy-start
  40.9 0.0 copy-start.1
  40.9 1.9 %block_scan.1 = (bf16[128,5,8,128]{3,2,1,0:T(8,128)(2,1)S(1)}, bf16[256,5120]{1,0:T(8,128)(2,1)S(1)}) custom-call(bf16[128,6,8,128]{3,2,1,0:T(8,128)(2,1)S(1)} %all-to-all-done.update_ref, bf16[256,5120]{1,0:T(8,128)(2,1)} %get-tuple-element.15.decayed_hbm), custom_call_target="tpu_custom_call" | custom-call | tf_op jit(solution)/shard_map/block_scan/pallas_call | solution.py:189
  42.9 25.9 %all_to_all.10.state_ref = bf16[128,5,8,128]{3,2,1,0:T(8,128)(2,1)S(1)} all-to-all(bf16[128,5,8,128]{3,2,1,0:T(8,128)(2,1)S(1)} %get-tuple-element.17), channel_id=1, replica_groups=mesh['seq'=32,'head'=4] {'seq','head'}, dimensions={0} | all-to-all | bytes 2621440 | tf_op jit(solution)/shard_map/all_to_all | solution.py:199
  68.7 0.0 copy-done
  68.7 0.0 copy-done.1
  68.7 2.6 %finish.1 = bf16[256,5120]{1,0:T(8,128)(2,1)} custom-call(bf16[256,5120]{1,0:T(8,128)(2,1)S(1)} %get-tuple-element.16.decayed_ref, bf16[128,5,8,128]{3,2,1,0:T(8,128)(2,1)S(1)} %all_to_all.10.state_ref, f32[256,5120]{1,0:T(8,128)S(1)} %copy-done, f32[1,5120]{1,0:T(1,128)S(1)} %bitcast.4), custom_call_target="tpu_custom_call" | custom-call | tf_op jit(solution)/shard_map/finish/pallas_call | solution.py:201
Async XLA Ops:
  4.1 36.9 %all-to-all-start = ((bf16[128,6,8,128]{3,2,1,0:T(8,128)(2,1)}), bf16[128,6,8,128]{3,2,1,0:T(8,128)(2,1)S(1)}, u32[]{:S(2)}, u32[]{:S(2)}) async-start(bf16[128,6,8,128]{3,2,1,0:T(8,128)(2,1)} %state_update.1), calls=%async_computation | async-start | bytes 3145728 | tf_op jit(solution)/shard_map/all_to_all | solution.py:165
  40.9 27.8 %copy-start = (f32[256,5120]{1,0:T(8,128)S(1)}, f32[256,5120]{1,0:T(8,128)}, u32[]{:S(2)}) copy-start(f32[256,5120]{1,0:T(8,128)} %get-tuple-element.18.within_ref) | copy-start | bytes 15728644
  40.9 27.8 %copy-start.1 = (f32[5120]{0:T(1024)S(1)}, f32[5120]{0:T(1024)}, u32[]{:S(2)}) copy-start(f32[5120]{0:T(1024)} %param.11) | copy-start | bytes 61444

commit v3 on v2

--- a/solution.py
+++ b/solution.py
@@ -15,6 +15,19 @@
 SLABS = 16
 DEVICES = GROUPS * SLABS
 STEP_GROUPS = 4
+ROWS = PER * 8 + 2
+
+
+def member_order():
+    order = []
+    for i in range(DEVICES):
+        bit = [(i >> k) & 1 for k in range(7)]
+        x, y, z = (bit[k] + 2 * bit[k + 4] for k in range(3))
+        order.append(((y * 4 + z) * 2 + bit[3]) * 4 + x)
+    return order
+
+
+ORDER = member_order()
 F32 = jnp.float32
 BF16 = jnp.bfloat16
 VMEM = 58 << 20
@@ -39,49 +52,64 @@
     return lax.dot_general(decay, tri, (((1,), (1,)), ((), ())), preferred_element_type=F32)
 
 
-def state_kernel(block_ref, key_ref, value_ref, decay_ref, docs_ref, out_ref, scale_ref, factor_ref):
+def state_kernel(block_ref, key_ref, value_ref, decay_ref, docs_ref, out_ref, scale_ref, wide_ref):
     step = pl.program_id(0)
 
     @pl.when(step == 0)
     def _():
         row, prev = doc_row(docs_ref, block_ref[0])
         last = row[:, BLOCK - 1 : BLOCK]
-        cum = cum_rows(decay_ref[...])
+        decay = decay_ref[...]
+        cum = cum_rows(decay)
         final = cum[:, BLOCK - 1 : BLOCK]
         same = (row == last).astype(F32)
         scale_ref[...] = jnp.exp(final - cum) * same
+        ones = jnp.ones((8, BLOCK), BF16)
+        final = lax.dot_general(ones, decay, (((1,), (1,)), ((), ())), preferred_element_type=F32)
         factor = jnp.exp(final) * (last == prev).astype(F32)
-        factor = jnp.broadcast_to(factor, (HEADS, DH))
         high = factor.astype(BF16).astype(F32)
         middle = (factor - high).astype(BF16).astype(F32)
         low = factor - high - middle
-        lane = lax.broadcasted_iota(jnp.int32, (HEADS, DH), 1)
-        parts = jnp.where(lane == 0, high, jnp.where(lane == 1, middle, jnp.where(lane == 2, low, 0.0)))
-        factor_ref[0:HEADS, :] = parts
-        factor_ref[HEADS:, :] = jnp.zeros((8, DH), F32)
+        parts = jnp.concatenate([high, middle, low, jnp.zeros((8, DH - 3 * HEADS), F32)], axis=1)
+        for piece in range(STEP_GROUPS * SLABS):
+            wide_ref[(piece + 1) * ROWS - 2 : (piece + 1) * ROWS, :] = parts[0:2]
 
     for sub in range(STEP_GROUPS):
         first = (step * STEP_GROUPS + sub) * PER
-        slabs = slice(sub * SLABS, (sub + 1) * SLABS)
+        start = sub * SLABS * ROWS
         for one in range(PER):
             cols = slice((sub * PER + one) * DH, (sub * PER + one + 1) * DH)
             keys = key_ref[:, cols].T.astype(F32)
             decayed = (keys * scale_ref[pl.ds(first + one, 1), :]).astype(BF16)
             update = jnp.dot(decayed, value_ref[:, cols], preferred_element_type=F32)
-            out_ref[slabs, one] = update.reshape(SLABS, 8, DH).astype(BF16)
-        parts = factor_ref[pl.ds(first, 8), :].astype(BF16)
-        out_ref[slabs, PER] = jnp.broadcast_to(parts[None], (SLABS, 8, DH))
-
-
-def scan_kernel(update_ref, decayed_hbm, out_ref, decayed_ref, sem):
+            for slab in range(SLABS):
+                at = start + slab * ROWS + one * 8
+                wide_ref[at : at + 8, :] = update[slab * 8 : (slab + 1) * 8]
+        rows = slice(start, start + SLABS * ROWS)
+        out_ref[rows, :] = wide_ref[rows, :].astype(BF16)
+
+
+def scan_kernel(block_ref, update_ref, decayed_hbm, out_ref, decayed_ref, wide_ref, factor_ref, sem):
     fetch = pltpu.make_async_copy(decayed_hbm, decayed_ref, sem)
     fetch.start()
+    for g in range(GROUPS):
+        rows = slice(g * SLABS * ROWS, (g + 1) * SLABS * ROWS)
+        wide_ref[rows, :] = update_ref[rows, :].astype(F32)
+    block = block_ref[0]
+    group = ((block >> 1) & 1) + 2 * ((block >> 6) & 1) + 4 * ((block >> 4) & 1)
+    parts = wide_ref[pl.ds(ROWS - 2, DEVICES, stride=ROWS), :].astype(BF16)
+    lane = lax.broadcasted_iota(jnp.int32, (DH, DH), 0)
+    for one in range(PER):
+        head = group * PER + one
+        pick = (lane == head) | (lane == head + HEADS) | (lane == head + 2 * HEADS)
+        factor_ref[one] = jnp.dot(parts, pick.astype(F32).astype(BF16), preferred_element_type=F32)
     state = [jnp.zeros((8, DH), F32) for _ in range(PER)]
     for b in range(DEVICES):
-        factors = jnp.sum(update_ref[b, PER].astype(F32), axis=1, keepdims=True)
+        place = ORDER.index(b)
         for one in range(PER):
-            out_ref[b, one] = state[one].astype(BF16)
-            state[one] = factors[one : one + 1] * state[one] + update_ref[b, one].astype(F32)
+            at = place * ROWS + one * 8
+            out_ref[place, one] = state[one].astype(BF16)
+            state[one] = factor_ref[one, place : place + 1, :] * state[one] + wide_ref[at : at + 8, :]
     fetch.wait()
 
 
@@ -147,22 +175,28 @@
     whole = lambda a: pl.BlockSpec(a.shape, lambda g, *_: (0,) * a.ndim)
 
     wider = pl.BlockSpec((BLOCK, STEP_GROUPS * wide), lambda g, *_: (0, g))
+    step_rows = STEP_GROUPS * SLABS * ROWS
     update = pl.pallas_call(
         state_kernel,
         grid_spec=pltpu.PrefetchScalarGridSpec(
             num_scalar_prefetch=1,
             grid=(GROUPS // STEP_GROUPS,),
             in_specs=[wider, wider, whole(decay), whole(docs)],
-            out_specs=pl.BlockSpec((STEP_GROUPS * SLABS, PER + 1, 8, DH), lambda g, *_: (g, 0, 0, 0)),
-            scratch_shapes=[pltpu.VMEM((HEADS, BLOCK), F32), pltpu.VMEM((HEADS + 8, DH), F32)],
+            out_specs=pl.BlockSpec((step_rows, DH), lambda g, *_: (g, 0)),
+            scratch_shapes=[pltpu.VMEM((HEADS, BLOCK), F32), pltpu.VMEM((step_rows, DH), F32)],
         ),
-        out_shape=jax.ShapeDtypeStruct((DEVICES, PER + 1, 8, DH), BF16),
+        out_shape=jax.ShapeDtypeStruct((DEVICES * ROWS, DH), BF16),
         compiler_params=pltpu.CompilerParams(vmem_limit_bytes=VMEM),
         cost_estimate=pl.CostEstimate(flops=340_000_000, bytes_accessed=7_000_000, transcendentals=10_000),
         name="state_update",
     )(block, keyed, valued, decay, docs)
 
-    moved = lax.all_to_all(update, axes, split_axis=0, concat_axis=0, tiled=True)
+    def exchange(pieces):
+        return lax.all_to_all(
+            pieces, axes, split_axis=0, concat_axis=0, axis_index_groups=[ORDER], tiled=True
+        )
+
+    moved = exchange(update.reshape(DEVICES, ROWS // 2, 2, DH)).reshape(DEVICES * ROWS, DH)
 
     within, decayed = pl.pallas_call(
         local_kernel,
@@ -188,15 +222,19 @@
     vmem = pl.BlockSpec(memory_space=pltpu.VMEM)
     states, decayed = pl.pallas_call(
         scan_kernel,
-        in_specs=[vmem, pl.BlockSpec(memory_space=pltpu.HBM)],
+        in_specs=[pl.BlockSpec(memory_space=pltpu.SMEM), vmem, pl.BlockSpec(memory_space=pltpu.HBM)],
         out_specs=[vmem, vmem],
         out_shape=[jax.ShapeDtypeStruct((DEVICES, PER, 8, DH), BF16), jax.ShapeDtypeStruct(query.shape, BF16)],
-        scratch_shapes=[pltpu.SemaphoreType.DMA],
-        compiler_params=pltpu.CompilerParams(vmem_limit_bytes=8 << 20),
+        scratch_shapes=[
+            pltpu.VMEM((DEVICES * ROWS, DH), F32),
+            pltpu.VMEM((PER, DEVICES, DH), F32),
+            pltpu.SemaphoreType.DMA,
+        ],
+        compiler_params=pltpu.CompilerParams(vmem_limit_bytes=16 << 20),
         name="block_scan",
-    )(moved, pltpu.with_memory_space_constraint(decayed, pltpu.HBM))
-
-    entering = lax.all_to_all(states, axes, split_axis=0, concat_axis=0, tiled=True)
+    )(block, moved, pltpu.with_memory_space_constraint(decayed, pltpu.HBM))
+
+    entering = exchange(states)
 
     return pl.pallas_call(
         finish_kernel,

time: 71.7 us -> 68.7 us (0.958)
  waiting for transfers between devices: 14.1 us -> 10.4 us
    all_to_all x1, waiting for transfers between devices: 14.1 us -> 10.4 us  [exchange(): lax.all_to_all(pieces, axes, split_axis=0, concat_axis=0, axis_index_grou...]
  transfers between devices with their start and end apart: 1 -> 1, of which waited for: 1 -> 1; matrix products, arithmetic and copies ran while one was open for 0% -> 0% of each run, Pallas kernels for 16% -> 17%
where the time goes in v3:
time: 68.7 us; the launch traced here: 68 us
  blocking collectives  26 us (38%)
  Pallas kernels  20.1 us (29%)
  starting transfers between devices  11.5 us (17%)
  waiting for transfers between devices  10.4 us (15%)
    all_to_all x1, blocking collectives, exchange(): lax.all_to_all(pieces, axes, split_axis=0, concat_axis=0, axis_index_grou...  26 us
    all_to_all x1, starting transfers between devices, exchange(): lax.all_to_all(pieces, axes, split_axis=0, concat_axis=0, axis_index_grou...  11.5 us
    pallas_call x1, Pallas kernels, body(): pl.pallas_call(local_kernel, grid_spec=pltpu.PrefetchScalarGridSpec(num_s...  11.3 us
    all_to_all x1, waiting for transfers between devices, exchange(): lax.all_to_all(pieces, axes, split_axis=0, concat_axis=0, axis_index_grou...  10.4 us
    pallas_call x1, Pallas kernels, body(): pl.pallas_call(state_kernel, grid_spec=pltpu.PrefetchScalarGridSpec(num_s...  4.31 us
    pallas_call x1, Pallas kernels, body(): pl.pallas_call(finish_kernel, in_specs=[vmem] * 4, out_specs=pl.BlockSpec...  2.57 us
    pallas_call x1, Pallas kernels, body(): pl.pallas_call(scan_kernel, in_specs=[pl.BlockSpec(memory_space=pltpu.SME...  1.91 us
  transfers between devices with their start and end apart: 1, of which 1 were waited for; matrix products, arithmetic and copies ran while one was open for 0% of the time, Pallas kernels for 17%

profile of v3, /device:TPU:1, one launch (start us, length us, event | category | flops | bytes accessed | tf_op | source)
XLA Modules:
  0.0 68.0 jit_solution(1794356700221839602)
XLA Ops:
  0.0 4.3 %state_update.1 = bf16[5376,128]{1,0:T(8,128)(2,1)} custom-call(s32[1]{0:T(128)} %bitcast.block_ref, bf16[256,5120]{1,0:T(8,128)(2,1)} %key_ref.3, bf16[256,5120]{1,0:T(8,128)(2,1)} %value_ref.3, bf16[40,256]{1,0:T(8,128)(2,1)} %bitcast.11, s32[256,128]{1,0:T(8,128)} %bitcast.9), custom_call_target="tpu_custom_call" | custom-call | flops 340000000 | bytes 7000000 | tf_op jit(solution)/shard_map/state_update/pallas_call | solution.py:179
  4.3 11.5 %all-to-all-start = ((bf16[128,21,2,128]{3,2,1,0:T(2,128)(2,1)}), bf16[128,21,2,128]{3,2,1,0:T(2,128)(2,1)S(1)}, u32[]{:S(2)}, u32[]{:S(2)}) async-start(bf16[128,21,2,128]{3,2,1,0:T(2,128)(2,1)} %bitcast.8), calls=%async_computation | async-start | bytes 2752512 | tf_op jit(solution)/shard_map/all_to_all | solution.py:195
  15.8 11.3 %local_attention.1 = (f32[256,5120]{1,0:T(8,128)}, bf16[256,5120]{1,0:T(8,128)(2,1)}) custom-call(s32[1]{0:T(128)} %bitcast.block_ref, bf16[256,5120]{1,0:T(8,128)(2,1)} %query_ref.1, bf16[256,5120]{1,0:T(8,128)(2,1)} %key_ref.3, bf16[256,5120]{1,0:T(8,128)(2,1)} %value_ref.3, bf16[40,256]{1,0:T(8,128)(2,1)} %bitcast.12, s32[256,128]{1,0:T(8,128)} %bitcast.10), custom_call_target="tpu_custom_call" | custom-call | flops 1400000000 | bytes 16000000 | tf_op jit(solution)/shard_map/local_attention/pallas_call | solution.py:201
  27.1 10.4 %all-to-all-done = bf16[128,21,2,128]{3,2,1,0:T(2,128)(2,1)S(1)} async-done(((bf16[128,21,2,128]{3,2,1,0:T(2,128)(2,1)}), bf16[128,21,2,128]{3,2,1,0:T(2,128)(2,1)S(1)}, u32[]{:S(2)}, u32[]{:S(2)}) %all-to-all-start) | async-done | bytes 1376288 | tf_op jit(solution)/shard_map/all_to_all | solution.py:195
  37.5 0.0 copy-start
  37.5 0.0 copy-start.1
  37.5 1.9 %block_scan.1 = (bf16[128,5,8,128]{3,2,1,0:T(8,128)(2,1)S(1)}, bf16[256,5120]{1,0:T(8,128)(2,1)S(1)}) custom-call(s32[1]{0:T(128)} %bitcast.block_ref, bf16[5376,128]{1,0:T(8,128)(2,1)S(1)} %bitcast.6, bf16[256,5120]{1,0:T(8,128)(2,1)} %get-tuple-element.15.decayed_hbm), custom_call_target="tpu_custom_call" | custom-call | tf_op jit(solution)/shard_map/block_scan/pallas_call | solution.py:223
  39.5 26.0 %all_to_all.10.state_ref = bf16[128,5,8,128]{3,2,1,0:T(8,128)(2,1)S(1)} all-to-all(bf16[128,5,8,128]{3,2,1,0:T(8,128)(2,1)S(1)} %get-tuple-element.17), channel_id=1, replica_groups={{0,1,32,33,8,9,40,41,4,5,36,37,12,13,44,45,2,3,34,35,10,11,42,43,6,7,38..., dimensions={0} | all-to-all | bytes 2621440 | tf_op jit(solution)/shard_map/all_to_all | solution.py:195
  65.5 0.0 copy-done
  65.5 0.0 copy-done.1
  65.5 2.6 %finish.1 = bf16[256,5120]{1,0:T(8,128)(2,1)} custom-call(bf16[256,5120]{1,0:T(8,128)(2,1)S(1)} %get-tuple-element.16.decayed_ref, bf16[128,5,8,128]{3,2,1,0:T(8,128)(2,1)S(1)} %all_to_all.10.state_ref, f32[256,5120]{1,0:T(8,128)S(1)} %copy-done, f32[1,5120]{1,0:T(1,128)S(1)} %bitcast.7), custom_call_target="tpu_custom_call" | custom-call | tf_op jit(solution)/shard_map/finish/pallas_call | solution.py:239
Async XLA Ops:
  4.3 33.2 %all-to-all-start = ((bf16[128,21,2,128]{3,2,1,0:T(2,128)(2,1)}), bf16[128,21,2,128]{3,2,1,0:T(2,128)(2,1)S(1)}, u32[]{:S(2)}, u32[]{:S(2)}) async-start(bf16[128,21,2,128]{3,2,1,0:T(2,128)(2,1)} %bitcast.8), calls=%async_computation | async-start | bytes 2752512 | tf_op jit(solution)/shard_map/all_to_all | solution.py:195
  37.5 27.9 %copy-start = (f32[256,5120]{1,0:T(8,128)S(1)}, f32[256,5120]{1,0:T(8,128)}, u32[]{:S(2)}) copy-start(f32[256,5120]{1,0:T(8,128)} %get-tuple-element.18.within_ref) | copy-start | bytes 15728644
  37.5 27.9 %copy-start.1 = (f32[5120]{0:T(1024)S(1)}, f32[5120]{0:T(1024)}, u32[]{:S(2)}) copy-start(f32[5120]{0:T(1024)} %param.11) | copy-start | bytes 61444

commit v4 on v3

--- a/solution.py
+++ b/solution.py
@@ -1,5 +1,3 @@
-import functools
-
 import jax
 import jax.numpy as jnp
 from jax import lax
@@ -16,18 +14,6 @@
 DEVICES = GROUPS * SLABS
 STEP_GROUPS = 4
 ROWS = PER * 8 + 2
-
-
-def member_order():
-    order = []
-    for i in range(DEVICES):
-        bit = [(i >> k) & 1 for k in range(7)]
-        x, y, z = (bit[k] + 2 * bit[k + 4] for k in range(3))
-        order.append(((y * 4 + z) * 2 + bit[3]) * 4 + x)
-    return order
-
-
-ORDER = member_order()
 F32 = jnp.float32
 BF16 = jnp.bfloat16
 VMEM = 58 << 20
@@ -92,24 +78,24 @@
 def scan_kernel(block_ref, update_ref, decayed_hbm, out_ref, decayed_ref, wide_ref, factor_ref, sem):
     fetch = pltpu.make_async_copy(decayed_hbm, decayed_ref, sem)
     fetch.start()
+    row = lax.broadcasted_iota(jnp.int32, (DH, PER * DH), 0)
+    column = lax.broadcasted_iota(jnp.int32, (DH, PER * DH), 1)
+    head = (block_ref[0] // SLABS) * PER + column // DH
+    pick = (row == head) | (row == head + HEADS) | (row == head + 2 * HEADS)
+    pick = pick.astype(F32).astype(BF16)
     for g in range(GROUPS):
-        rows = slice(g * SLABS * ROWS, (g + 1) * SLABS * ROWS)
+        first = g * SLABS * ROWS
+        rows = slice(first, first + SLABS * ROWS)
         wide_ref[rows, :] = update_ref[rows, :].astype(F32)
-    block = block_ref[0]
-    group = ((block >> 1) & 1) + 2 * ((block >> 6) & 1) + 4 * ((block >> 4) & 1)
-    parts = wide_ref[pl.ds(ROWS - 2, DEVICES, stride=ROWS), :].astype(BF16)
-    lane = lax.broadcasted_iota(jnp.int32, (DH, DH), 0)
-    for one in range(PER):
-        head = group * PER + one
-        pick = (lane == head) | (lane == head + HEADS) | (lane == head + 2 * HEADS)
-        factor_ref[one] = jnp.dot(parts, pick.astype(F32).astype(BF16), preferred_element_type=F32)
+        parts = wide_ref[pl.ds(first + ROWS - 2, SLABS, stride=ROWS), :].astype(BF16)
+        factor_ref[g * SLABS : (g + 1) * SLABS, :] = jnp.dot(parts, pick, preferred_element_type=F32)
     state = [jnp.zeros((8, DH), F32) for _ in range(PER)]
     for b in range(DEVICES):
-        place = ORDER.index(b)
         for one in range(PER):
-            at = place * ROWS + one * 8
-            out_ref[place, one] = state[one].astype(BF16)
-            state[one] = factor_ref[one, place : place + 1, :] * state[one] + wide_ref[at : at + 8, :]
+            at = b * ROWS + one * 8
+            out_ref[b, one] = state[one].astype(BF16)
+            factor = factor_ref[b : b + 1, one * DH : (one + 1) * DH]
+            state[one] = factor * state[one] + wide_ref[at : at + 8, :]
     fetch.wait()
 
 
@@ -192,9 +178,7 @@
     )(block, keyed, valued, decay, docs)
 
     def exchange(pieces):
-        return lax.all_to_all(
-            pieces, axes, split_axis=0, concat_axis=0, axis_index_groups=[ORDER], tiled=True
-        )
+        return lax.all_to_all(pieces, axes, split_axis=0, concat_axis=0, tiled=True)
 
     moved = exchange(update.reshape(DEVICES, ROWS // 2, 2, DH)).reshape(DEVICES * ROWS, DH)
 
@@ -227,7 +211,7 @@
         out_shape=[jax.ShapeDtypeStruct((DEVICES, PER, 8, DH), BF16), jax.ShapeDtypeStruct(query.shape, BF16)],
         scratch_shapes=[
             pltpu.VMEM((DEVICES * ROWS, DH), F32),
-            pltpu.VMEM((PER, DEVICES, DH), F32),
+            pltpu.VMEM((DEVICES, PER * DH), F32),
             pltpu.SemaphoreType.DMA,
         ],
         compiler_params=pltpu.CompilerParams(vmem_limit_bytes=16 << 20),

time: 68.7 us -> 69.8 us (1.016)
  waiting for transfers between devices: 10.4 us -> 12 us
    all_to_all x1, waiting for transfers between devices: 10.4 us -> 12 us  [exchange(): return lax.all_to_all(pieces, axes, split_axis=0, concat_axis=0, tiled=True)]
  transfers between devices with their start and end apart: 1 -> 1, of which waited for: 1 -> 1; matrix products, arithmetic and copies ran while one was open for 0% -> 0% of each run, Pallas kernels for 17% -> 16%
where the time goes in v4:
time: 69.8 us; the launch traced here: 69.4 us
  blocking collectives  25.9 us (37%)
  Pallas kernels  20.1 us (29%)
  waiting for transfers between devices  12 us (17%)
  starting transfers between devices  11.5 us (16%)
    all_to_all x1, blocking collectives, exchange(): return lax.all_to_all(pieces, axes, split_axis=0, concat_axis=0, tiled=True)  25.9 us
    all_to_all x1, waiting for transfers between devices, exchange(): return lax.all_to_all(pieces, axes, split_axis=0, concat_axis=0, tiled=True)  12 us
    all_to_all x1, starting transfers between devices, exchange(): return lax.all_to_all(pieces, axes, split_axis=0, concat_axis=0, tiled=True)  11.5 us
    pallas_call x1, Pallas kernels, body(): pl.pallas_call(local_kernel, grid_spec=pltpu.PrefetchScalarGridSpec(num_s...  11.3 us
    pallas_call x1, Pallas kernels, body(): pl.pallas_call(state_kernel, grid_spec=pltpu.PrefetchScalarGridSpec(num_s...  4.31 us
    pallas_call x1, Pallas kernels, body(): pl.pallas_call(finish_kernel, in_specs=[vmem] * 4, out_specs=pl.BlockSpec...  2.57 us
    pallas_call x1, Pallas kernels, body(): pl.pallas_call(scan_kernel, in_specs=[pl.BlockSpec(memory_space=pltpu.SME...  1.91 us
  transfers between devices with their start and end apart: 1, of which 1 were waited for; matrix products, arithmetic and copies ran while one was open for 0% of the time, Pallas kernels for 16%

profile of v4, /device:TPU:1, one launch (start us, length us, event | category | flops | bytes accessed | tf_op | source)
XLA Modules:
  0.0 69.4 jit_solution(13204541830557229764)
XLA Ops:
  0.0 4.3 %state_update.1 = bf16[5376,128]{1,0:T(8,128)(2,1)} custom-call(s32[1]{0:T(128)} %bitcast.block_ref, bf16[256,5120]{1,0:T(8,128)(2,1)} %key_ref.3, bf16[256,5120]{1,0:T(8,128)(2,1)} %value_ref.3, bf16[40,256]{1,0:T(8,128)(2,1)} %bitcast.11, s32[256,128]{1,0:T(8,128)} %bitcast.9), custom_call_target="tpu_custom_call" | custom-call | flops 340000000 | bytes 7000000 | tf_op jit(solution)/shard_map/state_update/pallas_call | solution.py:165
  4.3 11.5 %all-to-all-start = ((bf16[128,21,2,128]{3,2,1,0:T(2,128)(2,1)}), bf16[128,21,2,128]{3,2,1,0:T(2,128)(2,1)S(1)}, u32[]{:S(2)}, u32[]{:S(2)}) async-start(bf16[128,21,2,128]{3,2,1,0:T(2,128)(2,1)} %bitcast.8), calls=%async_computation | async-start | bytes 2752512 | tf_op jit(solution)/shard_map/all_to_all | solution.py:181
  15.8 11.3 %local_attention.1 = (f32[256,5120]{1,0:T(8,128)}, bf16[256,5120]{1,0:T(8,128)(2,1)}) custom-call(s32[1]{0:T(128)} %bitcast.block_ref, bf16[256,5120]{1,0:T(8,128)(2,1)} %query_ref.1, bf16[256,5120]{1,0:T(8,128)(2,1)} %key_ref.3, bf16[256,5120]{1,0:T(8,128)(2,1)} %value_ref.3, bf16[40,256]{1,0:T(8,128)(2,1)} %bitcast.12, s32[256,128]{1,0:T(8,128)} %bitcast.10), custom_call_target="tpu_custom_call" | custom-call | flops 1400000000 | bytes 16000000 | tf_op jit(solution)/shard_map/local_attention/pallas_call | solution.py:185
  27.1 12.0 %all-to-all-done = bf16[128,21,2,128]{3,2,1,0:T(2,128)(2,1)S(1)} async-done(((bf16[128,21,2,128]{3,2,1,0:T(2,128)(2,1)}), bf16[128,21,2,128]{3,2,1,0:T(2,128)(2,1)S(1)}, u32[]{:S(2)}, u32[]{:S(2)}) %all-to-all-start) | async-done | bytes 1376288 | tf_op jit(solution)/shard_map/all_to_all | solution.py:181
  39.1 0.0 copy-start
  39.1 0.0 copy-start.1
  39.1 1.9 %block_scan.1 = (bf16[128,5,8,128]{3,2,1,0:T(8,128)(2,1)S(1)}, bf16[256,5120]{1,0:T(8,128)(2,1)S(1)}) custom-call(s32[1]{0:T(128)} %bitcast.block_ref, bf16[5376,128]{1,0:T(8,128)(2,1)S(1)} %bitcast.6, bf16[256,5120]{1,0:T(8,128)(2,1)} %get-tuple-element.15.decayed_hbm), custom_call_target="tpu_custom_call" | custom-call | tf_op jit(solution)/shard_map/block_scan/pallas_call | solution.py:207
  41.0 25.9 %all_to_all.10.state_ref = bf16[128,5,8,128]{3,2,1,0:T(8,128)(2,1)S(1)} all-to-all(bf16[128,5,8,128]{3,2,1,0:T(8,128)(2,1)S(1)} %get-tuple-element.17), channel_id=1, replica_groups=mesh['seq'=32,'head'=4] {'seq','head'}, dimensions={0} | all-to-all | bytes 2621440 | tf_op jit(solution)/shard_map/all_to_all | solution.py:181
  66.8 0.0 copy-done
  66.9 0.0 copy-done.1
  66.9 2.6 %finish.1 = bf16[256,5120]{1,0:T(8,128)(2,1)} custom-call(bf16[256,5120]{1,0:T(8,128)(2,1)S(1)} %get-tuple-element.16.decayed_ref, bf16[128,5,8,128]{3,2,1,0:T(8,128)(2,1)S(1)} %all_to_all.10.state_ref, f32[256,5120]{1,0:T(8,128)S(1)} %copy-done, f32[1,5120]{1,0:T(1,128)S(1)} %bitcast.7), custom_call_target="tpu_custom_call" | custom-call | tf_op jit(solution)/shard_map/finish/pallas_call | solution.py:223
Async XLA Ops:
  4.3 34.8 %all-to-all-start = ((bf16[128,21,2,128]{3,2,1,0:T(2,128)(2,1)}), bf16[128,21,2,128]{3,2,1,0:T(2,128)(2,1)S(1)}, u32[]{:S(2)}, u32[]{:S(2)}) async-start(bf16[128,21,2,128]{3,2,1,0:T(2,128)(2,1)} %bitcast.8), calls=%async_computation | async-start | bytes 2752512 | tf_op jit(solution)/shard_map/all_to_all | solution.py:181
  39.1 27.8 %copy-start = (f32[256,5120]{1,0:T(8,128)S(1)}, f32[256,5120]{1,0:T(8,128)}, u32[]{:S(2)}) copy-start(f32[256,5120]{1,0:T(8,128)} %get-tuple-element.18.within_ref) | copy-start | bytes 15728644
  39.1 27.8 %copy-start.1 = (f32[5120]{0:T(1024)S(1)}, f32[5120]{0:T(1024)}, u32[]{:S(2)}) copy-start(f32[5120]{0:T(1024)} %param.11) | copy-start | bytes 61444

commit v5 on v4

--- a/solution.py
+++ b/solution.py
@@ -14,6 +14,18 @@
 DEVICES = GROUPS * SLABS
 STEP_GROUPS = 4
 ROWS = PER * 8 + 2
+
+
+def member_order():
+    order = []
+    for i in range(DEVICES):
+        bit = [(i >> k) & 1 for k in range(7)]
+        x, y, z = (bit[k] + 2 * bit[k + 4] for k in range(3))
+        order.append(((y * 4 + z) * 2 + bit[3]) * 4 + x)
+    return order
+
+
+ORDER = member_order()
 F32 = jnp.float32
 BF16 = jnp.bfloat16
 VMEM = 58 << 20
@@ -38,8 +50,9 @@
     return lax.dot_general(decay, tri, (((1,), (1,)), ((), ())), preferred_element_type=F32)
 
 
-def state_kernel(block_ref, key_ref, value_ref, decay_ref, docs_ref, out_ref, scale_ref, wide_ref):
+def state_kernel(block_ref, key_ref, value_ref, decay_ref, docs_ref, out_hbm, scale_ref, wide_ref, out_ref, sems):
     step = pl.program_id(0)
+    pair = 2 * SLABS * ROWS
 
     @pl.when(step == 0)
     def _():
@@ -72,15 +85,28 @@
                 at = start + slab * ROWS + one * 8
                 wide_ref[at : at + 8, :] = update[slab * 8 : (slab + 1) * 8]
         rows = slice(start, start + SLABS * ROWS)
-        out_ref[rows, :] = wide_ref[rows, :].astype(BF16)
+        at = step * (STEP_GROUPS * SLABS * ROWS) + start
+        out_ref[pl.ds(at, SLABS * ROWS), :] = wide_ref[rows, :].astype(BF16)
+        if sub % 2 == 1:
+            done = pl.ds(at - SLABS * ROWS, pair)
+            number = step * (STEP_GROUPS // 2) + sub // 2
+            pltpu.make_async_copy(out_ref.at[done], out_hbm.at[done], sems.at[number]).start()
+
+    @pl.when(step == GROUPS // STEP_GROUPS - 1)
+    def _():
+        for number in range(GROUPS // 2):
+            done = slice(number * pair, (number + 1) * pair)
+            pltpu.make_async_copy(out_ref.at[done], out_hbm.at[done], sems.at[number]).wait()
 
 
 def scan_kernel(block_ref, update_ref, decayed_hbm, out_ref, decayed_ref, wide_ref, factor_ref, sem):
     fetch = pltpu.make_async_copy(decayed_hbm, decayed_ref, sem)
     fetch.start()
+    block = block_ref[0]
+    group = ((block >> 1) & 1) + 2 * ((block >> 6) & 1) + 4 * ((block >> 4) & 1)
     row = lax.broadcasted_iota(jnp.int32, (DH, PER * DH), 0)
     column = lax.broadcasted_iota(jnp.int32, (DH, PER * DH), 1)
-    head = (block_ref[0] // SLABS) * PER + column // DH
+    head = group * PER + (column >> 7)
     pick = (row == head) | (row == head + HEADS) | (row == head + 2 * HEADS)
     pick = pick.astype(F32).astype(BF16)
     for g in range(GROUPS):
@@ -91,10 +117,11 @@
         factor_ref[g * SLABS : (g + 1) * SLABS, :] = jnp.dot(parts, pick, preferred_element_type=F32)
     state = [jnp.zeros((8, DH), F32) for _ in range(PER)]
     for b in range(DEVICES):
+        place = ORDER.index(b)
         for one in range(PER):
-            at = b * ROWS + one * 8
-            out_ref[b, one] = state[one].astype(BF16)
-            factor = factor_ref[b : b + 1, one * DH : (one + 1) * DH]
+            at = place * ROWS + one * 8
+            out_ref[place, one] = state[one].astype(BF16)
+            factor = factor_ref[place : place + 1, one * DH : (one + 1) * DH]
             state[one] = factor * state[one] + wide_ref[at : at + 8, :]
     fetch.wait()
 
@@ -168,8 +195,13 @@
             num_scalar_prefetch=1,
             grid=(GROUPS // STEP_GROUPS,),
             in_specs=[wider, wider, whole(decay), whole(docs)],
-            out_specs=pl.BlockSpec((step_rows, DH), lambda g, *_: (g, 0)),
-            scratch_shapes=[pltpu.VMEM((HEADS, BLOCK), F32), pltpu.VMEM((step_rows, DH), F32)],
+            out_specs=pl.BlockSpec(memory_space=pl.ANY),
+            scratch_shapes=[
+                pltpu.VMEM((HEADS, BLOCK), F32),
+                pltpu.VMEM((step_rows, DH), F32),
+                pltpu.VMEM((DEVICES * ROWS, DH), BF16),
+                pltpu.SemaphoreType.DMA((GROUPS // 2,)),
+            ],
         ),
         out_shape=jax.ShapeDtypeStruct((DEVICES * ROWS, DH), BF16),
         compiler_params=pltpu.CompilerParams(vmem_limit_bytes=VMEM),
@@ -178,7 +210,9 @@
     )(block, keyed, valued, decay, docs)
 
     def exchange(pieces):
-        return lax.all_to_all(pieces, axes, split_axis=0, concat_axis=0, tiled=True)
+        return lax.all_to_all(
+            pieces, axes, split_axis=0, concat_axis=0, axis_index_groups=[ORDER], tiled=True
+        )
 
     moved = exchange(update.reshape(DEVICES, ROWS // 2, 2, DH)).reshape(DEVICES * ROWS, DH)
 

time: 69.8 us -> 68.7 us (0.984)
  waiting for transfers between devices: 12 us -> 10.4 us
    all_to_all x1, waiting for transfers between devices: 12 us -> 10.4 us  [exchange(): lax.all_to_all(pieces, axes, split_axis=0, concat_axis=0, axis_index_grou...]
  transfers between devices with their start and end apart: 1 -> 1, of which waited for: 1 -> 1; matrix products, arithmetic and copies ran while one was open for 0% -> 0% of each run, Pallas kernels for 16% -> 17%
where the time goes in v5:
time: 68.7 us; the launch traced here: 67.9 us
  blocking collectives  26 us (38%)
  Pallas kernels  20 us (29%)
  starting transfers between devices  11.5 us (17%)
  waiting for transfers between devices  10.4 us (15%)
    all_to_all x1, blocking collectives, exchange(): lax.all_to_all(pieces, axes, split_axis=0, concat_axis=0, axis_index_grou...  26 us
    all_to_all x1, starting transfers between devices, exchange(): lax.all_to_all(pieces, axes, split_axis=0, concat_axis=0, axis_index_grou...  11.5 us
    pallas_call x1, Pallas kernels, body(): pl.pallas_call(local_kernel, grid_spec=pltpu.PrefetchScalarGridSpec(num_s...  11.3 us
    all_to_all x1, waiting for transfers between devices, exchange(): lax.all_to_all(pieces, axes, split_axis=0, concat_axis=0, axis_index_grou...  10.4 us
    pallas_call x1, Pallas kernels, body(): pl.pallas_call(state_kernel, grid_spec=pltpu.PrefetchScalarGridSpec(num_s...  4.2 us
    pallas_call x1, Pallas kernels, body(): pl.pallas_call(finish_kernel, in_specs=[vmem] * 4, out_specs=pl.BlockSpec...  2.57 us
    pallas_call x1, Pallas kernels, body(): pl.pallas_call(scan_kernel, in_specs=[pl.BlockSpec(memory_space=pltpu.SME...  1.91 us
  transfers between devices with their start and end apart: 1, of which 1 were waited for; matrix products, arithmetic and copies ran while one was open for 0% of the time, Pallas kernels for 17%

profile of v5, /device:TPU:1, one launch (start us, length us, event | category | flops | bytes accessed | tf_op | source)
XLA Modules:
  0.0 67.9 jit_solution(17050229061192377786)
XLA Ops:
  0.0 4.2 %state_update.1 = bf16[5376,128]{1,0:T(8,128)(2,1)} custom-call(s32[1]{0:T(128)} %bitcast.block_ref, bf16[256,5120]{1,0:T(8,128)(2,1)} %key_ref.3, bf16[256,5120]{1,0:T(8,128)(2,1)} %value_ref.3, bf16[40,256]{1,0:T(8,128)(2,1)} %bitcast.11, s32[256,128]{1,0:T(8,128)} %bitcast.9), custom_call_target="tpu_custom_call" | custom-call | flops 340000000 | bytes 7000000 | tf_op jit(solution)/shard_map/state_update/pallas_call | solution.py:192
  4.2 11.5 %all-to-all-start = ((bf16[128,21,2,128]{3,2,1,0:T(2,128)(2,1)}), bf16[128,21,2,128]{3,2,1,0:T(2,128)(2,1)S(1)}, u32[]{:S(2)}, u32[]{:S(2)}) async-start(bf16[128,21,2,128]{3,2,1,0:T(2,128)(2,1)} %bitcast.8), calls=%async_computation | async-start | bytes 2752512 | tf_op jit(solution)/shard_map/all_to_all | solution.py:213
  15.7 11.3 %local_attention.1 = (f32[256,5120]{1,0:T(8,128)}, bf16[256,5120]{1,0:T(8,128)(2,1)}) custom-call(s32[1]{0:T(128)} %bitcast.block_ref, bf16[256,5120]{1,0:T(8,128)(2,1)} %query_ref.1, bf16[256,5120]{1,0:T(8,128)(2,1)} %key_ref.3, bf16[256,5120]{1,0:T(8,128)(2,1)} %value_ref.3, bf16[40,256]{1,0:T(8,128)(2,1)} %bitcast.12, s32[256,128]{1,0:T(8,128)} %bitcast.10), custom_call_target="tpu_custom_call" | custom-call | flops 1400000000 | bytes 16000000 | tf_op jit(solution)/shard_map/local_attention/pallas_call | solution.py:219
  27.0 10.4 %all-to-all-done = bf16[128,21,2,128]{3,2,1,0:T(2,128)(2,1)S(1)} async-done(((bf16[128,21,2,128]{3,2,1,0:T(2,128)(2,1)}), bf16[128,21,2,128]{3,2,1,0:T(2,128)(2,1)S(1)}, u32[]{:S(2)}, u32[]{:S(2)}) %all-to-all-start) | async-done | bytes 1376288 | tf_op jit(solution)/shard_map/all_to_all | solution.py:213
  37.4 0.0 copy-start
  37.4 0.0 copy-start.1
  37.4 1.9 %block_scan.1 = (bf16[128,5,8,128]{3,2,1,0:T(8,128)(2,1)S(1)}, bf16[256,5120]{1,0:T(8,128)(2,1)S(1)}) custom-call(s32[1]{0:T(128)} %bitcast.block_ref, bf16[5376,128]{1,0:T(8,128)(2,1)S(1)} %bitcast.6, bf16[256,5120]{1,0:T(8,128)(2,1)} %get-tuple-element.15.decayed_hbm), custom_call_target="tpu_custom_call" | custom-call | tf_op jit(solution)/shard_map/block_scan/pallas_call | solution.py:241
  39.4 26.0 %all_to_all.10.state_ref = bf16[128,5,8,128]{3,2,1,0:T(8,128)(2,1)S(1)} all-to-all(bf16[128,5,8,128]{3,2,1,0:T(8,128)(2,1)S(1)} %get-tuple-element.17), channel_id=1, replica_groups={{0,1,32,33,8,9,40,41,4,5,36,37,12,13,44,45,2,3,34,35,10,11,42,43,6,7,38..., dimensions={0} | all-to-all | bytes 2621440 | tf_op jit(solution)/shard_map/all_to_all | solution.py:213
  65.4 0.0 copy-done
  65.4 0.0 copy-done.1
  65.4 2.6 %finish.1 = bf16[256,5120]{1,0:T(8,128)(2,1)} custom-call(bf16[256,5120]{1,0:T(8,128)(2,1)S(1)} %get-tuple-element.16.decayed_ref, bf16[128,5,8,128]{3,2,1,0:T(8,128)(2,1)S(1)} %all_to_all.10.state_ref, f32[256,5120]{1,0:T(8,128)S(1)} %copy-done, f32[1,5120]{1,0:T(1,128)S(1)} %bitcast.7), custom_call_target="tpu_custom_call" | custom-call | tf_op jit(solution)/shard_map/finish/pallas_call | solution.py:257
Async XLA Ops:
  4.2 33.2 %all-to-all-start = ((bf16[128,21,2,128]{3,2,1,0:T(2,128)(2,1)}), bf16[128,21,2,128]{3,2,1,0:T(2,128)(2,1)S(1)}, u32[]{:S(2)}, u32[]{:S(2)}) async-start(bf16[128,21,2,128]{3,2,1,0:T(2,128)(2,1)} %bitcast.8), calls=%async_computation | async-start | bytes 2752512 | tf_op jit(solution)/shard_map/all_to_all | solution.py:213
  37.4 27.9 %copy-start = (f32[256,5120]{1,0:T(8,128)S(1)}, f32[256,5120]{1,0:T(8,128)}, u32[]{:S(2)}) copy-start(f32[256,5120]{1,0:T(8,128)} %get-tuple-element.18.within_ref) | copy-start | bytes 15728644
  37.4 27.9 %copy-start.1 = (f32[5120]{0:T(1024)S(1)}, f32[5120]{0:T(1024)}, u32[]{:S(2)}) copy-start(f32[5120]{0:T(1024)} %param.11) | copy-start | bytes 61444

commit v6 on v5

--- a/solution.py
+++ b/solution.py
@@ -120,7 +120,7 @@
         place = ORDER.index(b)
         for one in range(PER):
             at = place * ROWS + one * 8
-            out_ref[place, one] = state[one].astype(BF16)
+            out_ref[b, one] = state[one].astype(BF16)
             factor = factor_ref[place : place + 1, one * DH : (one + 1) * DH]
             state[one] = factor * state[one] + wide_ref[at : at + 8, :]
     fetch.wait()
@@ -165,7 +165,8 @@
     for g in range(GROUPS):
         for one in range(g * PER, (g + 1) * PER):
             cols = slice(one * DH, (one + 1) * DH)
-            state = state_ref[g * SLABS : (g + 1) * SLABS, one - g * PER].reshape(DH, DH)
+            slabs = [state_ref[ORDER[g * SLABS + slab], one - g * PER] for slab in range(SLABS)]
+            state = jnp.stack(slabs).reshape(DH, DH)
             carried = jnp.dot(decayed_ref[:, cols], state, preferred_element_type=F32)
             total = within_ref[:, cols] + carried
             square = jnp.mean(total * total, axis=1, keepdims=True)
@@ -209,12 +210,12 @@
         name="state_update",
     )(block, keyed, valued, decay, docs)
 
-    def exchange(pieces):
+    def exchange(pieces, groups):
         return lax.all_to_all(
-            pieces, axes, split_axis=0, concat_axis=0, axis_index_groups=[ORDER], tiled=True
+            pieces, axes, split_axis=0, concat_axis=0, axis_index_groups=groups, tiled=True
         )
 
-    moved = exchange(update.reshape(DEVICES, ROWS // 2, 2, DH)).reshape(DEVICES * ROWS, DH)
+    moved = exchange(update.reshape(DEVICES, ROWS // 2, 2, DH), [ORDER]).reshape(DEVICES * ROWS, DH)
 
     within, decayed = pl.pallas_call(
         local_kernel,
@@ -252,7 +253,7 @@
         name="block_scan",
     )(block, moved, pltpu.with_memory_space_constraint(decayed, pltpu.HBM))
 
-    entering = exchange(states)
+    entering = exchange(states, None)
 
     return pl.pallas_call(
         finish_kernel,

time: 68.7 us -> 69.8 us (1.016)
  blocking collectives: 26 us -> 27.5 us
    all_to_all x1, blocking collectives: 26 us -> 27.5 us  [exchange(): lax.all_to_all(pieces, axes, split_axis=0, concat_axis=0, axis_index_grou...]
  transfers between devices with their start and end apart: 1 -> 1, of which waited for: 1 -> 1; matrix products, arithmetic and copies ran while one was open for 0% -> 0% of each run, Pallas kernels for 17% -> 16%
where the time goes in v6:
time: 69.8 us; the launch traced here: 69.4 us
  blocking collectives  27.5 us (39%)
  Pallas kernels  20 us (29%)
  starting transfers between devices  11.5 us (16%)
  waiting for transfers between devices  10.4 us (15%)
    all_to_all x1, blocking collectives, exchange(): lax.all_to_all(pieces, axes, split_axis=0, concat_axis=0, axis_index_grou...  27.5 us
    all_to_all x1, starting transfers between devices, exchange(): lax.all_to_all(pieces, axes, split_axis=0, concat_axis=0, axis_index_grou...  11.5 us
    pallas_call x1, Pallas kernels, body(): pl.pallas_call(local_kernel, grid_spec=pltpu.PrefetchScalarGridSpec(num_s...  11.3 us
    all_to_all x1, waiting for transfers between devices, exchange(): lax.all_to_all(pieces, axes, split_axis=0, concat_axis=0, axis_index_grou...  10.4 us
    pallas_call x1, Pallas kernels, body(): pl.pallas_call(state_kernel, grid_spec=pltpu.PrefetchScalarGridSpec(num_s...  4.2 us
    pallas_call x1, Pallas kernels, body(): pl.pallas_call(finish_kernel, in_specs=[vmem] * 4, out_specs=pl.BlockSpec...  2.57 us
    pallas_call x1, Pallas kernels, body(): pl.pallas_call(scan_kernel, in_specs=[pl.BlockSpec(memory_space=pltpu.SME...  1.91 us
  transfers between devices with their start and end apart: 1, of which 1 were waited for; matrix products, arithmetic and copies ran while one was open for 0% of the time, Pallas kernels for 16%

profile of v6, /device:TPU:1, one launch (start us, length us, event | category | flops | bytes accessed | tf_op | source)
XLA Modules:
  0.0 69.4 jit_solution(12767074473640745172)
XLA Ops:
  0.0 4.2 %state_update.1 = bf16[5376,128]{1,0:T(8,128)(2,1)} custom-call(s32[1]{0:T(128)} %bitcast.block_ref, bf16[256,5120]{1,0:T(8,128)(2,1)} %key_ref.3, bf16[256,5120]{1,0:T(8,128)(2,1)} %value_ref.3, bf16[40,256]{1,0:T(8,128)(2,1)} %bitcast.11, s32[256,128]{1,0:T(8,128)} %bitcast.9), custom_call_target="tpu_custom_call" | custom-call | flops 340000000 | bytes 7000000 | tf_op jit(solution)/shard_map/state_update/pallas_call | solution.py:193
  4.2 11.5 %all-to-all-start = ((bf16[128,21,2,128]{3,2,1,0:T(2,128)(2,1)}), bf16[128,21,2,128]{3,2,1,0:T(2,128)(2,1)S(1)}, u32[]{:S(2)}, u32[]{:S(2)}) async-start(bf16[128,21,2,128]{3,2,1,0:T(2,128)(2,1)} %bitcast.8), calls=%async_computation | async-start | bytes 2752512 | tf_op jit(solution)/shard_map/all_to_all | solution.py:214
  15.7 11.3 %local_attention.1 = (f32[256,5120]{1,0:T(8,128)}, bf16[256,5120]{1,0:T(8,128)(2,1)}) custom-call(s32[1]{0:T(128)} %bitcast.block_ref, bf16[256,5120]{1,0:T(8,128)(2,1)} %query_ref.1, bf16[256,5120]{1,0:T(8,128)(2,1)} %key_ref.3, bf16[256,5120]{1,0:T(8,128)(2,1)} %value_ref.3, bf16[40,256]{1,0:T(8,128)(2,1)} %bitcast.12, s32[256,128]{1,0:T(8,128)} %bitcast.10), custom_call_target="tpu_custom_call" | custom-call | flops 1400000000 | bytes 16000000 | tf_op jit(solution)/shard_map/local_attention/pallas_call | solution.py:220
  27.0 10.4 %all-to-all-done = bf16[128,21,2,128]{3,2,1,0:T(2,128)(2,1)S(1)} async-done(((bf16[128,21,2,128]{3,2,1,0:T(2,128)(2,1)}), bf16[128,21,2,128]{3,2,1,0:T(2,128)(2,1)S(1)}, u32[]{:S(2)}, u32[]{:S(2)}) %all-to-all-start) | async-done | bytes 1376288 | tf_op jit(solution)/shard_map/all_to_all | solution.py:214
  37.4 0.0 copy-start
  37.4 0.0 copy-start.1
  37.4 1.9 %block_scan.1 = (bf16[128,5,8,128]{3,2,1,0:T(8,128)(2,1)S(1)}, bf16[256,5120]{1,0:T(8,128)(2,1)S(1)}) custom-call(s32[1]{0:T(128)} %bitcast.block_ref, bf16[5376,128]{1,0:T(8,128)(2,1)S(1)} %bitcast.6, bf16[256,5120]{1,0:T(8,128)(2,1)} %get-tuple-element.15.decayed_hbm), custom_call_target="tpu_custom_call" | custom-call | tf_op jit(solution)/shard_map/block_scan/pallas_call | solution.py:242
  39.4 27.5 %all_to_all.10.state_ref = bf16[128,5,8,128]{3,2,1,0:T(8,128)(2,1)S(1)} all-to-all(bf16[128,5,8,128]{3,2,1,0:T(8,128)(2,1)S(1)} %get-tuple-element.17), channel_id=1, replica_groups=mesh['seq'=32,'head'=4] {'seq','head'}, dimensions={0} | all-to-all | bytes 2621440 | tf_op jit(solution)/shard_map/all_to_all | solution.py:214
  66.9 0.0 copy-done
  66.9 0.0 copy-done.1
  66.9 2.6 %finish.1 = bf16[256,5120]{1,0:T(8,128)(2,1)} custom-call(bf16[256,5120]{1,0:T(8,128)(2,1)S(1)} %get-tuple-element.16.decayed_ref, bf16[128,5,8,128]{3,2,1,0:T(8,128)(2,1)S(1)} %all_to_all.10.state_ref, f32[256,5120]{1,0:T(8,128)S(1)} %copy-done, f32[1,5120]{1,0:T(1,128)S(1)} %bitcast.7), custom_call_target="tpu_custom_call" | custom-call | tf_op jit(solution)/shard_map/finish/pallas_call | solution.py:258
Async XLA Ops:
  4.2 33.2 %all-to-all-start = ((bf16[128,21,2,128]{3,2,1,0:T(2,128)(2,1)}), bf16[128,21,2,128]{3,2,1,0:T(2,128)(2,1)S(1)}, u32[]{:S(2)}, u32[]{:S(2)}) async-start(bf16[128,21,2,128]{3,2,1,0:T(2,128)(2,1)} %bitcast.8), calls=%async_computation | async-start | bytes 2752512 | tf_op jit(solution)/shard_map/all_to_all | solution.py:214
  37.4 29.4 %copy-start = (f32[256,5120]{1,0:T(8,128)S(1)}, f32[256,5120]{1,0:T(8,128)}, u32[]{:S(2)}) copy-start(f32[256,5120]{1,0:T(8,128)} %get-tuple-element.18.within_ref) | copy-start | bytes 15728644
  37.4 29.4 %copy-start.1 = (f32[5120]{0:T(1024)S(1)}, f32[5120]{0:T(1024)}, u32[]{:S(2)}) copy-start(f32[5120]{0:T(1024)} %param.11) | copy-start | bytes 61444

commit v7 on v5

--- a/solution.py
+++ b/solution.py
@@ -20,8 +20,8 @@
     order = []
     for i in range(DEVICES):
         bit = [(i >> k) & 1 for k in range(7)]
-        x, y, z = (bit[k] + 2 * bit[k + 4] for k in range(3))
-        order.append(((y * 4 + z) * 2 + bit[3]) * 4 + x)
+        x, y, z = (bit[k] + 2 * bit[k + 3] for k in range(3))
+        order.append(((y * 4 + z) * 2 + bit[6]) * 4 + x)
     return order
 
 
@@ -103,7 +103,7 @@
     fetch = pltpu.make_async_copy(decayed_hbm, decayed_ref, sem)
     fetch.start()
     block = block_ref[0]
-    group = ((block >> 1) & 1) + 2 * ((block >> 6) & 1) + 4 * ((block >> 4) & 1)
+    group = ((block >> 6) & 1) + 2 * ((block >> 4) & 1) + 4 * ((block >> 2) & 1)
     row = lax.broadcasted_iota(jnp.int32, (DH, PER * DH), 0)
     column = lax.broadcasted_iota(jnp.int32, (DH, PER * DH), 1)
     head = group * PER + (column >> 7)

time: 68.7 us -> 70.5 us (1.026)
  waiting for transfers between devices: 10.4 us -> 12 us
    all_to_all x1, waiting for transfers between devices: 10.4 us -> 12 us  [exchange(): lax.all_to_all(pieces, axes, split_axis=0, concat_axis=0, axis_index_grou...]
  transfers between devices with their start and end apart: 1 -> 1, of which waited for: 1 -> 1; matrix products, arithmetic and copies ran while one was open for 0% -> 0% of each run, Pallas kernels for 17% -> 16%
where the time goes in v7:
time: 70.5 us; the launch traced here: 70.1 us
  blocking collectives  26.7 us (38%)
  Pallas kernels  20 us (28%)
  waiting for transfers between devices  12 us (17%)
  starting transfers between devices  11.5 us (16%)
    all_to_all x1, blocking collectives, exchange(): lax.all_to_all(pieces, axes, split_axis=0, concat_axis=0, axis_index_grou...  26.7 us
    all_to_all x1, waiting for transfers between devices, exchange(): lax.all_to_all(pieces, axes, split_axis=0, concat_axis=0, axis_index_grou...  12 us
    all_to_all x1, starting transfers between devices, exchange(): lax.all_to_all(pieces, axes, split_axis=0, concat_axis=0, axis_index_grou...  11.5 us
    pallas_call x1, Pallas kernels, body(): pl.pallas_call(local_kernel, grid_spec=pltpu.PrefetchScalarGridSpec(num_s...  11.3 us
    pallas_call x1, Pallas kernels, body(): pl.pallas_call(state_kernel, grid_spec=pltpu.PrefetchScalarGridSpec(num_s...  4.2 us
    pallas_call x1, Pallas kernels, body(): pl.pallas_call(finish_kernel, in_specs=[vmem] * 4, out_specs=pl.BlockSpec...  2.57 us
    pallas_call x1, Pallas kernels, body(): pl.pallas_call(scan_kernel, in_specs=[pl.BlockSpec(memory_space=pltpu.SME...  1.9 us
  transfers between devices with their start and end apart: 1, of which 1 were waited for; matrix products, arithmetic and copies ran while one was open for 0% of the time, Pallas kernels for 16%

profile of v7, /device:TPU:1, one launch (start us, length us, event | category | flops | bytes accessed | tf_op | source)
XLA Modules:
  0.0 70.1 jit_solution(1631275957334290716)
XLA Ops:
  0.0 4.2 %state_update.1 = bf16[5376,128]{1,0:T(8,128)(2,1)} custom-call(s32[1]{0:T(128)} %bitcast.block_ref, bf16[256,5120]{1,0:T(8,128)(2,1)} %key_ref.3, bf16[256,5120]{1,0:T(8,128)(2,1)} %value_ref.3, bf16[40,256]{1,0:T(8,128)(2,1)} %bitcast.11, s32[256,128]{1,0:T(8,128)} %bitcast.9), custom_call_target="tpu_custom_call" | custom-call | flops 340000000 | bytes 7000000 | tf_op jit(solution)/shard_map/state_update/pallas_call | solution.py:192
  4.2 11.5 %all-to-all-start = ((bf16[128,21,2,128]{3,2,1,0:T(2,128)(2,1)}), bf16[128,21,2,128]{3,2,1,0:T(2,128)(2,1)S(1)}, u32[]{:S(2)}, u32[]{:S(2)}) async-start(bf16[128,21,2,128]{3,2,1,0:T(2,128)(2,1)} %bitcast.8), calls=%async_computation | async-start | bytes 2752512 | tf_op jit(solution)/shard_map/all_to_all | solution.py:213
  15.7 11.3 %local_attention.1 = (f32[256,5120]{1,0:T(8,128)}, bf16[256,5120]{1,0:T(8,128)(2,1)}) custom-call(s32[1]{0:T(128)} %bitcast.block_ref, bf16[256,5120]{1,0:T(8,128)(2,1)} %query_ref.1, bf16[256,5120]{1,0:T(8,128)(2,1)} %key_ref.3, bf16[256,5120]{1,0:T(8,128)(2,1)} %value_ref.3, bf16[40,256]{1,0:T(8,128)(2,1)} %bitcast.12, s32[256,128]{1,0:T(8,128)} %bitcast.10), custom_call_target="tpu_custom_call" | custom-call | flops 1400000000 | bytes 16000000 | tf_op jit(solution)/shard_map/local_attention/pallas_call | solution.py:219
  27.0 12.0 %all-to-all-done = bf16[128,21,2,128]{3,2,1,0:T(2,128)(2,1)S(1)} async-done(((bf16[128,21,2,128]{3,2,1,0:T(2,128)(2,1)}), bf16[128,21,2,128]{3,2,1,0:T(2,128)(2,1)S(1)}, u32[]{:S(2)}, u32[]{:S(2)}) %all-to-all-start) | async-done | bytes 1376288 | tf_op jit(solution)/shard_map/all_to_all | solution.py:213
  39.0 0.0 copy-start
  39.0 0.0 copy-start.1
  39.0 1.9 %block_scan.1 = (bf16[128,5,8,128]{3,2,1,0:T(8,128)(2,1)S(1)}, bf16[256,5120]{1,0:T(8,128)(2,1)S(1)}) custom-call(s32[1]{0:T(128)} %bitcast.block_ref, bf16[5376,128]{1,0:T(8,128)(2,1)S(1)} %bitcast.6, bf16[256,5120]{1,0:T(8,128)(2,1)} %get-tuple-element.15.decayed_hbm), custom_call_target="tpu_custom_call" | custom-call | tf_op jit(solution)/shard_map/block_scan/pallas_call | solution.py:241
  40.9 26.7 %all_to_all.10.state_ref = bf16[128,5,8,128]{3,2,1,0:T(8,128)(2,1)S(1)} all-to-all(bf16[128,5,8,128]{3,2,1,0:T(8,128)(2,1)S(1)} %get-tuple-element.17), channel_id=1, replica_groups={{0,1,32,33,8,9,40,41,2,3,34,35,10,11,42,43,64,65,96,97,72,73,104,105,66..., dimensions={0} | all-to-all | bytes 2621440 | tf_op jit(solution)/shard_map/all_to_all | solution.py:213
  67.6 0.0 copy-done
  67.6 0.0 copy-done.1
  67.6 2.6 %finish.1 = bf16[256,5120]{1,0:T(8,128)(2,1)} custom-call(bf16[256,5120]{1,0:T(8,128)(2,1)S(1)} %get-tuple-element.16.decayed_ref, bf16[128,5,8,128]{3,2,1,0:T(8,128)(2,1)S(1)} %all_to_all.10.state_ref, f32[256,5120]{1,0:T(8,128)S(1)} %copy-done, f32[1,5120]{1,0:T(1,128)S(1)} %bitcast.7), custom_call_target="tpu_custom_call" | custom-call | tf_op jit(solution)/shard_map/finish/pallas_call | solution.py:257
Async XLA Ops:
  4.2 34.8 %all-to-all-start = ((bf16[128,21,2,128]{3,2,1,0:T(2,128)(2,1)}), bf16[128,21,2,128]{3,2,1,0:T(2,128)(2,1)S(1)}, u32[]{:S(2)}, u32[]{:S(2)}) async-start(bf16[128,21,2,128]{3,2,1,0:T(2,128)(2,1)} %bitcast.8), calls=%async_computation | async-start | bytes 2752512 | tf_op jit(solution)/shard_map/all_to_all | solution.py:213
  39.0 28.6 %copy-start = (f32[256,5120]{1,0:T(8,128)S(1)}, f32[256,5120]{1,0:T(8,128)}, u32[]{:S(2)}) copy-start(f32[256,5120]{1,0:T(8,128)} %get-tuple-element.18.within_ref) | copy-start | bytes 15728644
  39.0 28.6 %copy-start.1 = (f32[5120]{0:T(1024)S(1)}, f32[5120]{0:T(1024)}, u32[]{:S(2)}) copy-start(f32[5120]{0:T(1024)} %param.11) | copy-start | bytes 61444
